TPU v7x, 32 devices: a whole 2x2x4 slice. The times are simulated.
32 devices in a mesh: pass: 16 (over z, y, x), pb: 2 (over core).
Axes of the slice: x: 2, y: 2, z: 4, core: 2. Of those that a mesh axis runs over, the one named last changes fastest.
Arguments:
- hidden: bfloat16 [2, 16, 128, 768], P('pb', 'pass'), may hold values from -6 to 6
- encodings: bfloat16 [16, 2, 16, 128, 768], P('pass', 'pb'), may hold values from -6 to 6
- lengths: int32 [2, 16, 16], P('pb', 'pass'), may hold values from 32 to 128, as said below
- cotangent: bfloat16 [2, 16, 128, 768], P('pb', 'pass'), may hold values from -6 to 6
- self_query: bfloat16 [768, 768], replicated, may hold values from -0.0546875 to 0.0546875
- self_key: bfloat16 [768, 768], replicated, may hold values from -0.21875 to 0.21875
- self_value: bfloat16 [768, 768], replicated, may hold values from -0.21875 to 0.21875
- self_output: bfloat16 [768, 768], replicated, may hold values from -0.21875 to 0.21875
- cross_query: bfloat16 [768, 768], replicated, may hold values from -0.0546875 to 0.0546875
- cross_key: bfloat16 [768, 768], replicated, may hold values from -0.21875 to 0.21875
- cross_value: bfloat16 [768, 768], replicated, may hold values from -0.21875 to 0.21875
- cross_output: bfloat16 [768, 768], replicated, may hold values from -1.25 to 1.25
- feed_in: bfloat16 [768, 3072], replicated, may hold values from -0.21875 to 0.21875
- feed_out: bfloat16 [3072, 768], replicated, may hold values from -0.109375 to 0.109375
- gain_self: float32 [768], replicated, may hold values from 0.5 to 1.5
- gain_cross: float32 [768], replicated, may hold values from 0.5 to 1.5
- gain_feed: float32 [768], replicated, may hold values from 0.5 to 1.5
- bias_table: float32 [32, 12], replicated, may hold values from -4 to 4
Outputs:
- layer_out: float32 [2, 16, 128, 768], P('pb', 'pass')
- hidden_grad: float32 [2, 16, 128, 768], P('pb', 'pass')
- encodings_grad: bfloat16 [16, 2, 16, 128, 768], P('pass', 'pb')
- self_query_grad: float32 [768, 768], P('pass')
- self_key_grad: float32 [768, 768], P('pass')
- self_value_grad: float32 [768, 768], P('pass')
- self_output_grad: float32 [768, 768], P('pass')
- cross_query_grad: float32 [768, 768], P('pass')
- cross_key_grad: float32 [768, 768], P('pass')
- cross_value_grad: float32 [768, 768], P('pass')
- cross_output_grad: float32 [768, 768], P('pass')
- feed_in_grad: float32 [768, 3072], P('pass')
- feed_out_grad: float32 [3072, 768], P('pass')
- gain_self_grad: float32 [768], P('pass')
- gain_cross_grad: float32 [768], P('pass')
- gain_feed_grad: float32 [768], P('pass')
- bias_table_grad: float32 [32, 12], replicated
Inputs may be any that keep to these rules, and one draw needn't show every extreme that they name: `lengths`: every question has a passage of the full 128 slots.
All inputs are finite; a program needn't handle non-finite values.
Results may differ from a plain program's by a relative error of at most 0.023.
The roundings to bfloat16 on the way count: a program that leaves them out, or rounds other values in their place, can miss the bound.
Values may be sent and summed in bfloat16 or wider, within the bound.
A program may use at most 384 MiB of HBM per device.

v0:
```python
import jax
import jax.numpy as jnp
from jax import lax
from jax.sharding import PartitionSpec as P

HD = 64


EPS = 1e-06
LIMITS = (19, 21, 24, 27, 31, 35, 40, 46, 52, 59, 67, 77, 87, 99, 113)


def as_sent(shard):

    def short(part):
        return part.astype(jnp.bfloat16) if part.dtype == jnp.float32 else part

    return jax.tree.map(short, shard)


def narrow(value):
    return value.astype(jnp.bfloat16)


def product(left, right):
    return jnp.dot(left, right, preferred_element_type=jnp.float32)


def product_tn(left, right):
    return lax.dot_general(
        left, right, (((0,), (0,)), ((), ())), preferred_element_type=jnp.float32
    )


def product_nt(left, right):
    return lax.dot_general(
        left, right, (((1,), (1,)), ((), ())), preferred_element_type=jnp.float32
    )


def rms_norm(value, gain):
    scale = lax.rsqrt(jnp.mean(value * value, axis=-1, keepdims=True) + EPS)
    return value * scale * gain


def smooth(value):
    return jax.nn.gelu(value, approximate=True)


def bucket_onehot(length, count):
    places = jnp.arange(length, dtype=jnp.int32)
    distance = jnp.maximum(places[:, None] - places[None, :], 0)
    beyond = jnp.zeros_like(distance)
    for edge in LIMITS:
        beyond = beyond + (distance >= edge).astype(jnp.int32)
    bucket = jnp.where(distance < 16, distance, 16 + beyond)
    return (bucket[:, :, None] == jnp.arange(count, dtype=jnp.int32)[None, None, :]).astype(
        jnp.float32
    )


def head_slice(value, index):
    return lax.dynamic_slice_in_dim(value, index * HD, HD, 1)


def head_update(total, piece, index):
    return lax.dynamic_update_slice_in_dim(total, piece, index * HD, 1)


def head_chances(query_rows, key_rows, extra, allowed, index):
    scores = product_nt(head_slice(query_rows, index), head_slice(key_rows, index))
    scores = scores + lax.dynamic_index_in_dim(extra, index, 0, keepdims=False)
    scores = jnp.where(allowed, scores, -1e30)
    return jax.nn.softmax(scores, axis=-1)


def attend(query_rows, key_rows, value_rows, extra, allowed):
    heads = query_rows.shape[1] // HD

    def one_head(index, result):
        chances = narrow(head_chances(query_rows, key_rows, extra, allowed, index))
        return head_update(result, product(chances, head_slice(value_rows, index)), index)

    return lax.fori_loop(0, heads, one_head, jnp.zeros(query_rows.shape, jnp.float32))


def attend_back(query_rows, key_rows, value_rows, extra, allowed, grad_rows, keep_scores):
    heads = query_rows.shape[1] // HD
    if keep_scores:
        store = jnp.zeros((heads,) + allowed.shape, jnp.float32)
    else:
        store = jnp.zeros((heads, 1, 1), jnp.float32)

    def one_head(index, carry):
        grad_query, grad_key, grad_value, kept_scores = carry
        chances = head_chances(query_rows, key_rows, extra, allowed, index)
        grad_part = head_slice(grad_rows, index)
        grad_chances = product_nt(grad_part, head_slice(value_rows, index))
        grad_value = head_update(grad_value, product_tn(narrow(chances), grad_part), index)
        grad_scores = chances * (
            grad_chances - jnp.sum(chances * grad_chances, axis=-1, keepdims=True)
        )
        rounded = narrow(grad_scores)
        grad_query = head_update(grad_query, product(rounded, head_slice(key_rows, index)), index)
        grad_key = head_update(grad_key, product_tn(rounded, head_slice(query_rows, index)), index)
        if keep_scores:
            kept_scores = lax.dynamic_update_index_in_dim(kept_scores, grad_scores, index, 0)
        return (grad_query, grad_key, grad_value, kept_scores)

    start = (
        jnp.zeros(query_rows.shape, jnp.float32),
        jnp.zeros(key_rows.shape, jnp.float32),
        jnp.zeros(value_rows.shape, jnp.float32),
        store,
    )
    return lax.fori_loop(0, heads, one_head, start)


def forward(hidden_rows, cross_rows, valid, causal, position_bias, weights, gains):
    (
        self_query,
        self_key,
        self_value,
        self_output,
        cross_query,
        cross_key,
        cross_value,
        cross_output,
        feed_in,
        feed_out,
    ) = weights
    normed_one = narrow(rms_norm(hidden_rows, gains[0]))
    query_rows = narrow(product(normed_one, self_query))
    key_rows = narrow(product(normed_one, self_key))
    value_rows = narrow(product(normed_one, self_value))
    mixed_one = narrow(attend(query_rows, key_rows, value_rows, position_bias, causal))
    after_self = hidden_rows + product(mixed_one, self_output)
    normed_two = narrow(rms_norm(after_self, gains[1]))
    cross_queries = narrow(product(normed_two, cross_query))
    cross_keys = narrow(product(cross_rows, cross_key))
    cross_values = narrow(product(cross_rows, cross_value))
    flat_extra = jnp.zeros((self_query.shape[1] // HD, 1, 1), jnp.float32)
    mixed_two = narrow(attend(cross_queries, cross_keys, cross_values, flat_extra, valid))
    after_cross = after_self + product(mixed_two, cross_output)
    normed_three = narrow(rms_norm(after_cross, gains[2]))
    inner = product(normed_three, feed_in)
    active = narrow(smooth(inner))
    result = after_cross + product(active, feed_out)
    saved = (
        normed_one,
        query_rows,
        key_rows,
        value_rows,
        mixed_one,
        after_self,
        normed_two,
        cross_queries,
        cross_keys,
        cross_values,
        mixed_two,
        after_cross,
        normed_three,
        inner,
        active,
        cross_rows,
    )
    return (result, saved)


def per_device(
    hidden,
    encodings,
    lengths,
    cotangent,
    self_query,
    self_key,
    self_value,
    self_output,
    cross_query,
    cross_key,
    cross_value,
    cross_output,
    feed_in,
    feed_out,
    gain_self,
    gain_cross,
    gain_feed,
    bias_table,
):
    answer_tokens = hidden.shape[2]
    model_width = hidden.shape[3]
    slot_size = encodings.shape[3]
    passages = lengths.shape[2]
    hidden_rows = hidden.reshape(answer_tokens, model_width).astype(jnp.float32)
    length_row = lengths.reshape(passages)
    slot_places = jnp.arange(slot_size, dtype=jnp.int32)
    valid = (slot_places[None, :] < length_row[:, None]).reshape(1, passages * slot_size)
    places = jnp.arange(answer_tokens, dtype=jnp.int32)
    causal = places[:, None] >= places[None, :]
    onehot = bucket_onehot(answer_tokens, bias_table.shape[0])
    position_bias = jnp.einsum(
        "qkb,bh->hqk",
        onehot,
        bias_table,
        precision=lax.Precision.HIGHEST,
        preferred_element_type=jnp.float32,
    )
    weights = (
        self_query,
        self_key,
        self_value,
        self_output,
        cross_query,
        cross_key,
        cross_value,
        cross_output,
        feed_in,
        feed_out,
    )
    gains = (gain_self, gain_cross, gain_feed)
    heads = model_width // HD
    gathered = lax.all_to_all(encodings, "pass", split_axis=2, concat_axis=0, tiled=True)
    cross_rows = gathered.reshape(passages * slot_size, model_width)
    result, saved = forward(hidden_rows, cross_rows, valid, causal, position_bias, weights, gains)
    again = lax.all_to_all(encodings, "pass", split_axis=2, concat_axis=0, tiled=True)
    unused, saved = forward(
        hidden_rows,
        again.reshape(passages * slot_size, model_width),
        valid,
        causal,
        position_bias,
        weights,
        gains,
    )
    (
        normed_one,
        query_rows,
        key_rows,
        value_rows,
        mixed_one,
        after_self,
        normed_two,
        cross_queries,
        cross_keys,
        cross_values,
        mixed_two,
        after_cross,
        normed_three,
        inner,
        active,
        source_rows,
    ) = saved
    upstream = cotangent.reshape(answer_tokens, model_width).astype(jnp.float32)
    branch_feed = narrow(upstream)
    grad_feed_out = product_tn(active, branch_feed)
    grad_active = product_nt(branch_feed, feed_out)
    unused, smooth_pull = jax.vjp(smooth, inner)
    grad_inner = narrow(smooth_pull(grad_active)[0])
    grad_feed_in = product_tn(normed_three, grad_inner)
    unused, norm_pull = jax.vjp(rms_norm, after_cross, gain_feed)
    back_rows, grad_gain_feed = norm_pull(product_nt(grad_inner, feed_in))
    grad_cross = upstream + back_rows
    branch_cross = narrow(grad_cross)
    grad_cross_output = product_tn(mixed_two, branch_cross)
    grad_mixed = narrow(product_nt(branch_cross, cross_output))
    flat_extra = jnp.zeros((heads, 1, 1), jnp.float32)
    grad_query, grad_key, grad_value, unused = attend_back(
        cross_queries, cross_keys, cross_values, flat_extra, valid, grad_mixed, False
    )
    grad_query = narrow(grad_query)
    grad_key = narrow(grad_key)
    grad_value = narrow(grad_value)
    grad_cross_query = product_tn(normed_two, grad_query)
    grad_cross_key = product_tn(source_rows, grad_key)
    grad_cross_value = product_tn(source_rows, grad_value)
    grad_source = narrow(product_nt(grad_key, cross_key) + product_nt(grad_value, cross_value))
    returned = lax.all_to_all(
        grad_source.reshape(passages, 1, 1, slot_size, model_width),
        "pass",
        split_axis=0,
        concat_axis=2,
        tiled=True,
    )
    unused, norm_pull = jax.vjp(rms_norm, after_self, gain_cross)
    back_rows, grad_gain_cross = norm_pull(product_nt(grad_query, cross_query))
    grad_self = grad_cross + back_rows
    branch_self = narrow(grad_self)
    grad_self_output = product_tn(mixed_one, branch_self)
    grad_mixed = narrow(product_nt(branch_self, self_output))
    grad_query, grad_key, grad_value, score_grads = attend_back(
        query_rows, key_rows, value_rows, position_bias, causal, grad_mixed, True
    )
    grad_query = narrow(grad_query)
    grad_key = narrow(grad_key)
    grad_value = narrow(grad_value)
    grad_self_query = product_tn(normed_one, grad_query)
    grad_self_key = product_tn(normed_one, grad_key)
    grad_self_value = product_tn(normed_one, grad_value)
    into_norm = (
        product_nt(grad_query, self_query)
        + product_nt(grad_key, self_key)
        + product_nt(grad_value, self_value)
    )
    unused, norm_pull = jax.vjp(rms_norm, hidden_rows, gain_self)
    back_rows, grad_gain_self = norm_pull(into_norm)
    grad_hidden = grad_self + back_rows
    grad_table = jnp.einsum(
        "hqk,qkb->bh",
        score_grads,
        onehot,
        precision=lax.Precision.HIGHEST,
        preferred_element_type=jnp.float32,
    )
    shares = (
        lax.psum_scatter(grad_self_query, "pass", scatter_dimension=0, tiled=True),
        lax.psum_scatter(grad_self_key, "pass", scatter_dimension=0, tiled=True),
        lax.psum_scatter(grad_self_value, "pass", scatter_dimension=0, tiled=True),
        lax.psum_scatter(grad_self_output, "pass", scatter_dimension=0, tiled=True),
        lax.psum_scatter(grad_cross_query, "pass", scatter_dimension=0, tiled=True),
        lax.psum_scatter(grad_cross_key, "pass", scatter_dimension=0, tiled=True),
        lax.psum_scatter(grad_cross_value, "pass", scatter_dimension=0, tiled=True),
        lax.psum_scatter(grad_cross_output, "pass", scatter_dimension=0, tiled=True),
        lax.psum_scatter(grad_feed_in, "pass", scatter_dimension=0, tiled=True),
        lax.psum_scatter(grad_feed_out, "pass", scatter_dimension=0, tiled=True),
        lax.psum_scatter(grad_gain_self, "pass", scatter_dimension=0, tiled=True),
        lax.psum_scatter(grad_gain_cross, "pass", scatter_dimension=0, tiled=True),
        lax.psum_scatter(grad_gain_feed, "pass", scatter_dimension=0, tiled=True),
    )
    totals = jax.tree.map(
        lambda part: part.astype(jnp.float32), lax.psum(as_sent(tuple(shares)), "pb")
    )
    table_sum = lax.psum(grad_table, ("pass", "pb"))
    return (
        (result.reshape(hidden.shape), grad_hidden.reshape(hidden.shape), returned)
        + tuple(totals)
        + (table_sum,)
    )


def solution(mesh):
    in_specs = (
        P("pb", "pass", None, None),
        P("pass", "pb", None, None, None),
        P("pb", "pass", None),
        P("pb", "pass", None, None),
        P(),
        P(),
        P(),
        P(),
        P(),
        P(),
        P(),
        P(),
        P(),
        P(),
        P(),
        P(),
        P(),
        P(),
    )
    out_specs = (
        P("pb", "pass", None, None),
        P("pb", "pass", None, None),
        P("pass", "pb", None, None, None),
        P("pass", None),
        P("pass", None),
        P("pass", None),
        P("pass", None),
        P("pass", None),
        P("pass", None),
        P("pass", None),
        P("pass", None),
        P("pass", None),
        P("pass", None),
        P("pass"),
        P("pass"),
        P("pass"),
        P(),
    )
    return jax.shard_map(
        per_device, mesh=mesh, in_specs=in_specs, out_specs=out_specs, check_vma=False
    )
```

profile of v0, /device:TPU:13, one launch (start us, length us, event | category | flops | bytes accessed | tf_op | source)
XLA Modules:
  0.0 1878.7 jit_solution(502211889615562113)
XLA Ops:
  7.2 6.8 all-to-all-start
  24.9 32.4 %while.76 = (s32[]{:T(128)}, bf16[128,768]{0,1:T(8,128)(2,1)}, bf16[128,768]{1,0:T(8,128)(2,1)}, bf16[128,768]{1,0:T(8,128)(2,1)S(1)}, f32[12,128,128]{1,2,0:T(8...) while((s32[]{:T(128)}, bf16[128,768]{0,1:T(8,128)(2,1)}, ...), condition=%wide.region_4.5_spmd.clone, body=%wide.region_1.4_spmd.clone.sunk | while | flops 4341510 | bytes 398483 | solution.py:84
  60.6 23.8 %all-to-all-done = bf16[1,1,16,128,768]{4,3,1,0,2:T(8,128)(2,1)} async-done(((bf16[1,1,16,128,768]{4,3,1,0,2:T(8,128)(2,1)}), bf16[1,1,16,128,768]{4,3,1,0,2:T(8,128)(2,1)}, u32[]{:S(2)}, u32[]{:S(2)}) %all-to-all-start) | async-done | bytes 3145760 | tf_op jit(solution)/shard_map/all_to_all | solution.py:222
  84.3 6.2 convolution_convert_fusion
  90.5 6.2 convolution_convert_fusion.1
  96.7 43.7 %while.77 = (s32[]{:T(128)}, bf16[128,768]{0,1:T(8,128)(2,1)S(1)}, bf16[128,768]{1,0:T(8,128)(2,1)S(1)}, bf16[2048,768]{1,0:T(8,128)(2,1)}, bf16[2048,768]{1,0:T...) while((s32[]{:T(128)}, bf16[128,768]{0,1:T(8,128)(2,1)S(1)}, ...), condition=%wide.region_9.10_spmd.clone, body=%wide.region_6.9_spmd.clone.sunk | while | flops 68945664 | bytes 4268755 | solution.py:84
  143.2 3.3 fusion.135
  146.6 4.8 fusion.68
  161.1 118.2 %while.78 = (s32[]{:T(128)}, bf16[128,768]{0,1:T(8,128)(2,1)}, bf16[2048,768]{0,1:T(8,128)(2,1)}, bf16[2048,768]{0,1:T(8,128)(2,1)}, bf16[128,768]{1,0:T(8,128)(...) while((s32[]{:T(128)}, bf16[128,768]{0,1:T(8,128)(2,1)}, ...), condition=%wide.region_16.17_spmd.clone, body=%wide.region_12.16_spmd.clone.sunk | while | flops 171968128 | bytes 11713259 | solution.py:116
  291.1 104.4 %while.79 = (s32[]{:T(128)}, bf16[128,768]{0,1:T(8,128)(2,1)S(1)}, bf16[128,768]{0,1:T(8,128)(2,1)}, bf16[128,768]{0,1:T(8,128)(2,1)}, f32[12,128,128]{1,0,2:T(8...) while((s32[]{:T(128)}, bf16[128,768]{0,1:T(8,128)(2,1)S(1)}, ...), condition=%wide.region_22.23_spmd.clone, body=%wide.region_18.22_spmd.clone.sunk | while | flops 10796678 | bytes 1191095 | solution.py:116
  404.0 6.9 convolution_bitcast_fusion.1
  414.1 6.8 convolution_bitcast_fusion
  427.5 5.1 fusion.134
  434.0 5.2 fusion.85
  439.3 4.8 fusion.146
  444.1 4.2 add_convert_fusion
  448.3 5.0 all-to-all-start.1
  459.4 118.0 %reduce-scatter.21.cloned.1.call-done = f32[48,768]{1,0:T(8,128)} async-done(((f32[768,768]{1,0:T(8,128)}), f32[48,768]{1,0:T(8,128)}) %reduce-scatter.21.cloned.1.call-update) | async-done | bytes 147472 | tf_op jit(solution)/shard_map/reduce_scatter | solution.py:318
  579.0 130.8 %reduce-scatter.15.cloned.1.call-done = f32[48,768]{1,0:T(8,128)} async-done(((f32[768,768]{1,0:T(8,128)}), f32[48,768]{1,0:T(8,128)}) %reduce-scatter.15.cloned.1.call-update) | async-done | bytes 147472 | tf_op jit(solution)/shard_map/reduce_scatter | solution.py:315
  711.3 131.6 %reduce-scatter.17.cloned.1.call-done = f32[48,768]{1,0:T(8,128)} async-done(((f32[768,768]{1,0:T(8,128)}), f32[48,768]{1,0:T(8,128)}) %reduce-scatter.17.cloned.1.call-update) | async-done | bytes 147472 | tf_op jit(solution)/shard_map/reduce_scatter | solution.py:316
  844.4 130.6 %reduce-scatter.19.cloned.1.call-done = f32[48,768]{1,0:T(8,128)} async-done(((f32[768,768]{1,0:T(8,128)}), f32[48,768]{1,0:T(8,128)}) %reduce-scatter.19.cloned.1.call-update) | async-done | bytes 147472 | tf_op jit(solution)/shard_map/reduce_scatter | solution.py:317
  976.6 131.6 %reduce-scatter.31.cloned.1.call-done = f32[48,768]{1,0:T(8,128)} async-done(((f32[768,768]{1,0:T(8,128)}), f32[48,768]{1,0:T(8,128)}) %reduce-scatter.31.cloned.1.call-update) | async-done | bytes 147472
  1109.9 130.9 %reduce-scatter.33.cloned.1.call-done = f32[48,768]{1,0:T(8,128)} async-done(((f32[768,768]{1,0:T(8,128)}), f32[48,768]{1,0:T(8,128)}) %reduce-scatter.33.cloned.1.call-update) | async-done | bytes 147472
  1242.5 131.6 %reduce-scatter.25.cloned.1.call-done = f32[48,768]{1,0:T(8,128)} async-done(((f32[768,768]{1,0:T(8,128)}), f32[48,768]{1,0:T(8,128)}) %reduce-scatter.25.cloned.1.call-update) | async-done | bytes 147472 | tf_op jit(solution)/shard_map/reduce_scatter | solution.py:322
  1375.6 174.5 %reduce-scatter.27.cloned.1.call-done = f32[48,3072]{1,0:T(8,128)} async-done(((f32[768,3072]{1,0:T(8,128)}), f32[48,3072]{1,0:T(8,128)}) %reduce-scatter.27.cloned.1.call-update) | async-done | bytes 589840 | tf_op jit(solution)/shard_map/reduce_scatter | solution.py:323
  1551.9 174.6 %reduce-scatter.29.cloned.1.call-done = f32[192,768]{1,0:T(8,128)} async-done(((f32[3072,768]{1,0:T(8,128)}), f32[192,768]{1,0:T(8,128)}) %reduce-scatter.29.cloned.1.call-update) | async-done | bytes 589840 | tf_op jit(solution)/shard_map/reduce_scatter | solution.py:324
  1728.4 3.2 fusion.78
  1731.6 51.7 %all-reduce.3 = (bf16[768]{0:T(1024)(128)(2,1)S(1)}, bf16[768]{0:T(1024)(128)(2,1)S(1)}, bf16[768]{0:T(1024)(128)(2,1)S(1)}) all-reduce(f32[768]{0:T(1024)S(1)} %get-tuple-element.774, f32[768]{0:T(1024)S(1)} %copy-done.42, f32[768]{0:T(1024)} %get-tuple-element.770), channel_id=12, replica_groups=mesh['pass'=16,'pb'=2] {'pass'}, use_global_device_ids=true, to_apply=%region_45.46.clone | all-reduce | flops 2304 | bytes 13824
  1783.5 17.4 all-reduce.4
  1804.9 47.0 %psum.111 = f32[32,12]{0,1:T(8,128)} all-reduce(f32[32,12]{0,1:T(8,128)S(1)} %convolution_bitcast_fusion.3), channel_id=1, replica_groups=mesh['pass'=16,'pb'=2] {'pass','pb'}, use_global_device_ids=true, to_apply=%region_53.54 | all-reduce | flops 384 | bytes 3072 | tf_op jit(solution)/shard_map/psum | solution.py:332
  1854.6 4.1 fusion.74
  1868.1 3.8 copy.125
  (484 shorter events, 391.6 us)
Async XLA Ops:
  7.2 83.3 %copy-start = (bf16[768,768]{1,0:T(8,128)(2,1)S(1)}, bf16[768,768]{1,0:T(8,128)(2,1)}, u32[]{:S(2)}) copy-start(bf16[768,768]{1,0:T(8,128)(2,1)} %param.35) | copy-start | bytes 3538948
  7.2 7.0 copy-start.1
  7.2 7.1 copy-start.28
  7.2 77.1 %all-to-all-start = ((bf16[1,1,16,128,768]{4,3,1,0,2:T(8,128)(2,1)}), bf16[1,1,16,128,768]{4,3,1,0,2:T(8,128)(2,1)}, u32[]{:S(2)}, u32[]{:S(2)}) async-start(bf16[1,1,16,128,768]{4,3,1,0,2:T(8,128)(2,1)} %bitcast.117), calls=%async_computation | async-start | bytes 6291456 | tf_op jit(solution)/shard_map/all_to_all | solution.py:222
  14.0 443.9 %reduce-scatter.23.cloned.1.call-start = ((), (), s32[]{:S(2)}) async-start(), calls=%async_computation.16 | async-start | bytes 2506752 | tf_op jit(solution)/shard_map/reduce_scatter | solution.py:319
  22.6 35.6 %copy-start.7 = (bf16[768,768]{1,0:T(8,128)(2,1)S(1)}, bf16[768,768]{1,0:T(8,128)(2,1)}, u32[]{:S(2)}) copy-start(bf16[768,768]{1,0:T(8,128)(2,1)} %param.33) | copy-start | bytes 3538948
  59.7 24.6 %copy-start.50 = (bf16[768,768]{1,0:T(8,128)(2,1)S(1)}, bf16[768,768]{1,0:T(8,128)(2,1)}, u32[]{:S(2)}) copy-start(bf16[768,768]{1,0:T(8,128)(2,1)} %param.36) | copy-start | bytes 3538948
  60.2 30.3 %copy-start.46 = (f32[128]{0:T(128)}, f32[128]{0:T(128)S(1)}, u32[]{:S(2)}) copy-start(f32[128]{0:T(128)S(1)} %fusion.132) | copy-start | bytes 1540
  90.5 6.2 copy-start.39
  96.7 45.1 %copy-start.5 = (bf16[768,768]{1,0:T(8,128)(2,1)S(1)}, bf16[768,768]{1,0:T(8,128)(2,1)}, u32[]{:S(2)}) copy-start(bf16[768,768]{1,0:T(8,128)(2,1)} %param.37) | copy-start | bytes 3538948
  143.2 10.6 copy-start.43
  143.2 8.2 slice-start
  282.2 295.2 %reduce-scatter.21.cloned.1.call-start = ((), (), s32[]{:S(2)}) async-start(), calls=%async_computation.15 | async-start | bytes 2506752 | tf_op jit(solution)/shard_map/reduce_scatter | solution.py:318
  289.6 420.2 %reduce-scatter.15.cloned.1.call-start = ((), (), s32[]{:S(2)}) async-start(), calls=%async_computation.12 | async-start | bytes 2506752 | tf_op jit(solution)/shard_map/reduce_scatter | solution.py:315
  398.2 444.7 %reduce-scatter.17.cloned.1.call-start = ((), (), s32[]{:S(2)}) async-start(), calls=%async_computation.13 | async-start | bytes 2506752 | tf_op jit(solution)/shard_map/reduce_scatter | solution.py:316
  401.1 574.0 %reduce-scatter.19.cloned.1.call-start = ((), (), s32[]{:S(2)}) async-start(), calls=%async_computation.14 | async-start | bytes 2506752 | tf_op jit(solution)/shard_map/reduce_scatter | solution.py:317
  404.0 704.2 %reduce-scatter.31.cloned.1.call-start = ((), (), s32[]{:S(2)}) async-start(), calls=%async_computation.20 | async-start | bytes 2506752
  414.0 826.8 %reduce-scatter.33.cloned.1.call-start = ((), (), s32[]{:S(2)}) async-start(), calls=%async_computation.21 | async-start | bytes 2506752
  424.0 950.1 %reduce-scatter.25.cloned.1.call-start = ((), (), s32[]{:S(2)}) async-start(), calls=%async_computation.17 | async-start | bytes 2506752 | tf_op jit(solution)/shard_map/reduce_scatter | solution.py:322
  426.8 1123.3 %reduce-scatter.27.cloned.1.call-start = ((), (), s32[]{:S(2)}) async-start(), calls=%async_computation.18 | async-start | bytes 10027008 | tf_op jit(solution)/shard_map/reduce_scatter | solution.py:323
  432.6 1293.9 %reduce-scatter.29.cloned.1.call-start = ((), (), s32[]{:S(2)}) async-start(), calls=%async_computation.19 | async-start | bytes 10027008 | tf_op jit(solution)/shard_map/reduce_scatter | solution.py:324
  448.3 5.1 copy-start.52
  448.3 6.3 copy-start.17
  448.3 1410.4 %all-to-all-start.1 = ((bf16[16,1,1,128,768]{4,3,2,1,0:T(8,128)(2,1)}), bf16[16,1,1,128,768]{4,3,2,1,0:T(8,128)(2,1)}, u32[]{:S(2)}, u32[]{:S(2)}) async-start(bf16[16,1,1,128,768]{4,3,2,1,0:T(8,128)(2,1)} %bitcast.118), calls=%async_computation.1 | async-start | bytes 6291456 | tf_op jit(solution)/shard_map/all_to_all | solution.py:277
  453.3 1405.4 %all-reduce.8.cloned.1.call-start = ((), (), s32[]{:S(2)}) async-start(), calls=%async_computation.22 | async-start | bytes 2850816 | tf_op jit(solution)/shard_map/psum | solution.py:330
  1375.6 352.7 %copy-start.21 = (bf16[128,768]{0,1:T(8,128)(2,1)S(1)}, bf16[128,768]{0,1:T(8,128)(2,1)}, u32[]{:S(2)}) copy-start(bf16[128,768]{0,1:T(8,128)(2,1)} %get-tuple-element.628) | copy-start | bytes 589828
  1858.7 5.1 copy-start.35
  1858.7 5.8 copy-start.34
  1858.8 6.5 copy-start.33
  1858.8 7.1 copy-start.32
  1858.8 7.8 copy-start.31
  1858.8 8.6 copy-start.30
  (36 other events, 83.0 us)
Sparse Core Ops, SparseCore 0:
  282.4 126.8 reduce-scatter.22
  415.0 162.4 reduce-scatter.20
  582.4 127.3 reduce-scatter.14
  715.3 127.5 reduce-scatter.16
  847.7 127.3 reduce-scatter.18
  980.6 127.5 reduce-scatter.30
  1113.1 127.6 reduce-scatter.32
  1246.5 127.5 reduce-scatter.24
  1379.8 170.2 reduce-scatter.26
  1556.6 169.9 reduce-scatter.28
  1730.8 22.3 all-reduce.7
where the time goes:
time: 1890 us; the launch traced here: 1880 us
  waiting for transfers between devices  1280 us (68%)
  matrix products  343 us (18%)
  blocking collectives  116 us (6%)
  local copies, waits for them, and re-layouts  70.7 us (4%)
  other arithmetic  41.4 us (2%)
    unnamed x13, waiting for transfers between devices  263 us
    reduce_scatter x1, waiting for transfers between devices, per_device(): lax.psum_scatter(grad_feed_out, 'pass', scatter_dimension=0, tiled=True)  175 us
    reduce_scatter x1, waiting for transfers between devices, per_device(): lax.psum_scatter(grad_feed_in, 'pass', scatter_dimension=0, tiled=True)  174 us
    reduce_scatter x1, waiting for transfers between devices, per_device(): lax.psum_scatter(grad_self_key, 'pass', scatter_dimension=0, tiled=True)  132 us
    reduce_scatter x1, waiting for transfers between devices, per_device(): lax.psum_scatter(grad_cross_output, 'pass', scatter_dimension=0, tiled=True)  132 us
    reduce_scatter x1, waiting for transfers between devices, per_device(): lax.psum_scatter(grad_self_query, 'pass', scatter_dimension=0, tiled=True)  131 us
    reduce_scatter x1, waiting for transfers between devices, per_device(): lax.psum_scatter(grad_self_value, 'pass', scatter_dimension=0, tiled=True)  131 us
    dot_general x82, matrix products, product_nt(): lax.dot_general(left, right, (((1,), (1,)), ((), ())), preferred_element_...  121 us
  transfers between devices with their start and end apart: 13, of which 10 were waited for; matrix products, arithmetic and copies ran while one was open for 13% of the time, Pallas kernels for 0%

commit v1 on v0

v1 whole, which is shorter than its diff:
```python
import functools

import jax
import jax.numpy as jnp
import numpy as np
from jax import lax
from jax.experimental import pallas as pl
from jax.experimental.pallas import tpu as pltpu
from jax.sharding import PartitionSpec as P

HD = 64
EPS = 1e-06
LIMITS = (19, 21, 24, 27, 31, 35, 40, 46, 52, 59, 67, 77, 87, 99, 113)
NEG = -1e30
BF = jnp.bfloat16
F32 = jnp.float32
MESH = pl.DeviceIdType.MESH
ROOT = 0.7978845608028654
VMEM_LIMIT = 56 << 20


def narrow(value):
    return value.astype(BF)


def dot_nn(left, right):
    return lax.dot_general(left, right, (((1,), (0,)), ((), ())), preferred_element_type=F32)


def dot_nt(left, right):
    return lax.dot_general(left, right, (((1,), (1,)), ((), ())), preferred_element_type=F32)


def dot_tn(left, right):
    return lax.dot_general(left, right, (((0,), (0,)), ((), ())), preferred_element_type=F32)


def rms(value, gain):
    scale = lax.rsqrt(jnp.mean(value * value, axis=-1, keepdims=True) + EPS)
    return value * scale * gain


def rms_back(value, gain, grad):
    scale = lax.rsqrt(jnp.mean(value * value, axis=-1, keepdims=True) + EPS)
    scaled = grad * gain
    inner = jnp.mean(scaled * value, axis=-1, keepdims=True)
    rows = scaled * scale - value * (scale * scale * scale * inner)
    gain_grad = jnp.sum(grad * (value * scale), axis=0, keepdims=True)
    return rows, gain_grad


def pair_mask(pair):
    lane = lax.broadcasted_iota(jnp.int32, pair.shape, 1)
    zero = jnp.zeros_like(pair)
    return jnp.concatenate(
        [jnp.where(lane < HD, pair, zero), jnp.where(lane >= HD, pair, zero)], axis=0
    )


def pair_diag(both, rows):
    return jnp.concatenate([both[:HD, :rows], both[HD:, rows:]], axis=0)


def bucket_onehot_rows(buckets, length):
    distance = lax.broadcasted_iota(jnp.int32, (buckets, length), 1)
    row = lax.broadcasted_iota(jnp.int32, (buckets, length), 0)
    beyond = jnp.zeros_like(distance)
    for edge in LIMITS:
        beyond = beyond + (distance >= edge).astype(jnp.int32)
    bucket = jnp.where(distance < 16, distance, 16 + beyond)
    return (bucket == row).astype(F32)


def head_bias(table, rows):
    onehot = bucket_onehot_rows(table.shape[0], rows)
    return lax.dot_general(
        table, onehot, (((0,), (0,)), ((), ())), precision=lax.Precision.HIGHEST,
        preferred_element_type=F32,
    )


def toeplitz(row, rows):
    return pltpu.roll(jnp.broadcast_to(row, (rows, rows)), 0, 1, stride=1, stride_axis=0)


def diagonal_sums(square):
    rows = square.shape[0]
    place = lax.broadcasted_iota(jnp.int32, square.shape, 0)
    for bit in range(3):
        moved = pltpu.roll(square, rows - (1 << bit), 1)
        square = jnp.where((place >> bit) & 1 == 1, moved, square)
    total = square[:8]
    for group in range(1, rows // 8):
        total = total + pltpu.roll(square[8 * group : 8 * group + 8], rows - 8 * group, 1)
    return jnp.sum(total, axis=0, keepdims=True)


def causal_mask(rows):
    key = lax.broadcasted_iota(jnp.int32, (rows, 2 * rows), 0)
    query = lax.broadcasted_iota(jnp.int32, (rows, 2 * rows), 1)
    query = jnp.where(query >= rows, query - rows, query)
    return key <= query


def self_forward_kernel(
    hidden, wq, wk, wv, wo, wcq, g1, g2, table,
    h1_out, q_out, k_out, v_out, mix_out, after_out, h2_out, cq_out,
):
    rows, width = hidden.shape
    pairs = width // (2 * HD)
    value = hidden[...].astype(F32)
    h1 = narrow(rms(value, g1[...]))
    h1_out[...] = h1
    q = narrow(dot_nn(h1, wq[...]))
    k = narrow(dot_nn(h1, wk[...]))
    v = narrow(dot_nn(h1, wv[...]))
    q_out[...] = q
    k_out[...] = k
    v_out[...] = v
    bias = head_bias(table[...], rows)
    allowed = causal_mask(rows)
    mixed = []
    for pair in range(pairs):
        at = slice(pair * 2 * HD, (pair + 1) * 2 * HD)
        scores = dot_nt(k[:, at], pair_mask(q[:, at]))
        both = jnp.concatenate(
            [toeplitz(bias[2 * pair : 2 * pair + 1], rows), toeplitz(bias[2 * pair + 1 : 2 * pair + 2], rows)],
            axis=1,
        )
        scores = jnp.where(allowed, scores + both, NEG)
        top = jnp.max(scores, axis=0, keepdims=True)
        raised = jnp.exp(scores - top)
        chances = raised / jnp.sum(raised, axis=0, keepdims=True)
        mixed.append(pair_diag(dot_tn(v[:, at], narrow(chances)), rows))
    mix = narrow(jnp.concatenate(mixed, axis=0).T)
    mix_out[...] = mix
    after = value + dot_nn(mix, wo[...])
    after_out[...] = after
    h2 = narrow(rms(after, g2[...]))
    h2_out[...] = h2
    cq_out[...] = narrow(dot_nn(h2, wcq[...]))


def cross_forward_kernel(slot, lengths, enc, wk, wv, cq, k_out, v_out, mix_out, lse_out, masked, top, total, acc):
    step = pl.program_id(0)
    rows, width = cq.shape
    block = enc.shape[0]
    pairs = width // (2 * HD)

    @pl.when(step == 0)
    def _():
        for pair in range(pairs):
            at = slice(pair * 2 * HD, (pair + 1) * 2 * HD)
            masked[pair] = pair_mask(cq[:, at])
        top[...] = jnp.full(top.shape, NEG, F32)
        total[...] = jnp.zeros(total.shape, F32)
        acc[...] = jnp.zeros(acc.shape, F32)

    source = enc[...]
    k_out[...] = narrow(dot_nn(source, wk[...]))
    v_out[...] = narrow(dot_nn(source, wv[...]))
    place = lax.broadcasted_iota(jnp.int32, (slot, 2 * rows), 0)
    passages = block // slot
    valid = jnp.concatenate([place < lengths[step * passages + i] for i in range(passages)], axis=0)
    for pair in range(pairs):
        at = slice(pair * 2 * HD, (pair + 1) * 2 * HD)
        scores = jnp.where(valid, dot_nt(k_out[:, at], masked[pair]), NEG)
        before = top[pair : pair + 1]
        now = jnp.maximum(before, jnp.max(scores, axis=0, keepdims=True))
        top[pair : pair + 1] = now
        fade = jnp.exp(before - now)
        raised = jnp.exp(scores - now)
        total[pair : pair + 1] = total[pair : pair + 1] * fade + jnp.sum(raised, axis=0, keepdims=True)
        part = pair_diag(dot_tn(v_out[:, at], narrow(raised)), rows)
        fades = jnp.concatenate(
            [jnp.broadcast_to(fade[:, :rows], (HD, rows)), jnp.broadcast_to(fade[:, rows:], (HD, rows))], axis=0
        )
        acc[at, :] = acc[at, :] * fades + part

    @pl.when(step == pl.num_programs(0) - 1)
    def _():
        for pair in range(pairs):
            at = slice(pair * 2 * HD, (pair + 1) * 2 * HD)
            sums = total[pair : pair + 1]
            lse_out[pair : pair + 1] = top[pair : pair + 1] + jnp.log(sums)
            inverse = 1.0 / sums
            spread = jnp.concatenate(
                [jnp.broadcast_to(inverse[:, :rows], (HD, rows)), jnp.broadcast_to(inverse[:, rows:], (HD, rows))],
                axis=0,
            )
            mix_out[at, :] = acc[at, :] * spread


def feed_kernel(
    mix_t, after_self, cot, wo, w_in, w_out, g3,
    result_out, grad_out, gmix_out, delta_out, dgain_out, d_in, d_out, d_o,
):
    rows, width = cot.shape
    hidden_units = w_in.shape[1]
    mix = narrow(mix_t[...].T)
    after = after_self[...] + dot_nn(mix, wo[...])
    h3 = narrow(rms(after, g3[...]))
    inner = dot_nn(h3, w_in[...])
    bent = jnp.tanh(ROOT * (inner + 0.044715 * (inner * inner * inner)))
    active = narrow(0.5 * inner * (1.0 + bent))
    result_out[...] = after + dot_nn(active, w_out[...])
    cb = cot[...]
    d_out[...] = narrow(dot_tn(active, cb))
    slope = 0.5 * (1.0 + bent) + (0.5 * ROOT) * inner * (1.0 - bent * bent) * (1.0 + (3 * 0.044715) * inner * inner)
    gi = narrow(dot_nt(cb, w_out[...]) * slope)
    pieces = hidden_units // width
    for piece in range(pieces):
        d_in[piece] = narrow(dot_tn(h3, gi[:, piece * width : (piece + 1) * width]))
    back, gain_grad = rms_back(after, g3[...], dot_nt(gi, w_in[...]))
    dgain_out[...] = gain_grad
    grad = cb.astype(F32) + back
    grad_out[...] = grad
    gb = narrow(grad)
    d_o[...] = narrow(dot_tn(mix, gb))
    gmix = narrow(dot_nt(gb, wo[...]))
    gmix_out[...] = gmix
    product = gmix.astype(F32).T * mix_t[...]
    for pair in range(width // (2 * HD)):
        first = jnp.sum(product[pair * 2 * HD : pair * 2 * HD + HD], axis=0, keepdims=True)
        second = jnp.sum(product[pair * 2 * HD + HD : (pair + 1) * 2 * HD], axis=0, keepdims=True)
        delta_out[pair : pair + 1] = jnp.concatenate([first, second], axis=1)


def cross_backward_kernel(
    slot, lengths, enc, k, v, wk, wv, cq, gmix, lse, delta,
    enc_out, dq_out, dk_out, dv_out, masked, gmasked, dq_t, dkv, acc,
):
    step = pl.program_id(0)
    rows, width = cq.shape
    block = enc.shape[0]
    pairs = width // (2 * HD)

    @pl.when(step == 0)
    def _():
        for pair in range(pairs):
            at = slice(pair * 2 * HD, (pair + 1) * 2 * HD)
            masked[pair] = pair_mask(cq[:, at])
            gmasked[pair] = pair_mask(gmix[:, at])
        dq_t[...] = jnp.zeros(dq_t.shape, F32)
        acc[...] = jnp.zeros(acc.shape, F32)

    place = lax.broadcasted_iota(jnp.int32, (slot, 2 * rows), 0)
    passages = block // slot
    valid = jnp.concatenate([place < lengths[step * passages + i] for i in range(passages)], axis=0)
    for pair in range(pairs):
        at = slice(pair * 2 * HD, (pair + 1) * 2 * HD)
        scores = jnp.where(valid, dot_nt(k[:, at], masked[pair]), NEG)
        chances = jnp.exp(scores - lse[pair : pair + 1])
        dkv[:, width + pair * 2 * HD : width + (pair + 1) * 2 * HD] = narrow(dot_nn(narrow(chances), gmasked[pair]))
        ds = narrow(chances * (dot_nt(v[:, at], gmasked[pair]) - delta[pair : pair + 1]))
        dkv[:, at] = narrow(dot_nn(ds, masked[pair]))
        dq_t[at, :] = dq_t[at, :] + pair_diag(dot_tn(k[:, at], ds), rows)
    enc_out[...] = narrow(dot_nt(dkv[:, :width], wk[...]) + dot_nt(dkv[:, width:], wv[...]))
    acc[...] = acc[...] + dot_tn(enc[...], dkv[...])

    @pl.when(step == pl.num_programs(0) - 1)
    def _():
        dq_out[...] = narrow(dq_t[...].T)
        dk_out[...] = narrow(acc[:, :width])
        dv_out[...] = narrow(acc[:, width:])


def self_backward_kernel(
    hidden, h1, q, k, v, mix, after_self, h2, dcq, grad_cross, wq, wk, wv, wo, wcq, g1, g2, table,
    hidden_out, d_cq, d_o, d_q, d_k, d_v, dg1_out, dg2_out, dtable_out,
):
    rows, width = hidden.shape
    pairs = width // (2 * HD)
    d_cq[...] = narrow(dot_tn(h2[...], dcq[...]))
    back, gain_grad = rms_back(after_self[...], g2[...], dot_nt(dcq[...], wcq[...]))
    dg2_out[...] = gain_grad
    grad = grad_cross[...] + back
    sb = narrow(grad)
    d_o[...] = narrow(dot_tn(mix[...], sb))
    gmix = narrow(dot_nt(sb, wo[...]))
    bias = head_bias(table[...], rows)
    allowed = causal_mask(rows)
    dq_parts, dk_parts, dv_parts, sums = [], [], [], []
    for pair in range(pairs):
        at = slice(pair * 2 * HD, (pair + 1) * 2 * HD)
        masked = pair_mask(q[:, at])
        gmasked = pair_mask(gmix[:, at])
        scores = dot_nt(k[:, at], masked)
        both = jnp.concatenate(
            [toeplitz(bias[2 * pair : 2 * pair + 1], rows), toeplitz(bias[2 * pair + 1 : 2 * pair + 2], rows)],
            axis=1,
        )
        scores = jnp.where(allowed, scores + both, NEG)
        top = jnp.max(scores, axis=0, keepdims=True)
        raised = jnp.exp(scores - top)
        chances = raised / jnp.sum(raised, axis=0, keepdims=True)
        dv_parts.append(narrow(dot_nn(narrow(chances), gmasked)))
        dp = dot_nt(v[:, at], gmasked)
        ds = chances * (dp - jnp.sum(chances * dp, axis=0, keepdims=True))
        sums.append(diagonal_sums(ds[:, :rows]))
        sums.append(diagonal_sums(ds[:, rows:]))
        dsb = narrow(ds)
        dk_parts.append(narrow(dot_nn(dsb, masked)))
        dq_parts.append(pair_diag(dot_tn(k[:, at], dsb), rows))
    dq = narrow(jnp.concatenate(dq_parts, axis=0).T)
    dk = jnp.concatenate(dk_parts, axis=1)
    dv = jnp.concatenate(dv_parts, axis=1)
    d_q[...] = narrow(dot_tn(h1[...], dq))
    d_k[...] = narrow(dot_tn(h1[...], dk))
    d_v[...] = narrow(dot_tn(h1[...], dv))
    into = dot_nt(dq, wq[...]) + dot_nt(dk, wk[...]) + dot_nt(dv, wv[...])
    back, gain_grad = rms_back(hidden[...].astype(F32), g1[...], into)
    dg1_out[...] = gain_grad
    hidden_out[...] = grad + back
    by_distance = jnp.concatenate(sums, axis=0)
    onehot = bucket_onehot_rows(table.shape[0], rows)
    dtable_out[...] = lax.dot_general(
        onehot, by_distance, (((1,), (1,)), ((), ())), precision=lax.Precision.HIGHEST, preferred_element_type=F32
    )


def add_rows(left, right, dest):
    count = dest.shape[0]

    def one(index, carry):
        dest[index] = narrow(left[index].astype(F32) + right[index].astype(F32))
        return carry

    lax.fori_loop(0, count, one, 0)


def reduce_kernel(n, singles, grouped, *refs):
    pieces = singles + grouped
    ins = list(refs[:singles]) + [refs[singles].at[:, i] for i in range(grouped)]
    small_in, out, small_out = refs[singles + 1 : singles + 4]
    bits = n.bit_length() - 1
    scratch = refs[singles + 4 :]
    mine, other, stages = scratch[0], scratch[1], scratch[2 : 2 + bits]
    local_sem, send_sem, recv_sem, small_buf, small_send, small_recv, last_sem = scratch[2 + bits : 9 + bits]
    half = pieces // 2
    me, core = lax.axis_index("pass"), lax.axis_index("pb")
    partner = (me, 1 - core)

    barrier = pltpu.get_barrier_semaphore()
    pl.semaphore_signal(barrier, inc=1, device_id=partner, device_id_type=MESH)
    for bit in range(bits):
        pl.semaphore_signal(barrier, inc=1, device_id=(me ^ (1 << bit), core), device_id_type=MESH)
    pl.semaphore_wait(barrier, bits + 1)

    def remote(src, dst, send, recv, device):
        return pltpu.make_async_remote_copy(
            src_ref=src, dst_ref=dst, send_sem=send, recv_sem=recv, device_id=device, device_id_type=MESH
        )

    def order(piece):
        first = list(range(bits))
        if piece % 2 and bits > 1:
            first[0], first[1] = first[1], first[0]
        return first

    def split(ref, piece, stage):
        done = order(piece)[:stage]
        bit = order(piece)[stage]
        low = 1 << len([b for b in range(bit) if b not in done])
        count = n >> stage
        view = ref.reshape(count // (2 * low), 2, low, ref.shape[-2], ref.shape[-1])
        return view, (me >> bit) & 1, low, count // (2 * low), bit

    def swap(i, c):
        return remote(ins[2 * i + 1 - c], other.at[i], send_sem.at[i, 0], recv_sem.at[i, 0], partner)

    def fetch(i, c):
        return pltpu.make_async_copy(ins[2 * i + c], mine.at[i], local_sem.at[i])

    for i in range(half):
        for c in range(2):

            @pl.when(core == c)
            def _(i=i, c=c):
                swap(i, c).start()
                fetch(i, c).start()

    def source(i, stage):
        return other.at[i] if stage == 0 else stages[stage - 1].at[i]

    def stage_copy(i, stage):
        view, value, low, high, bit = split(source(i, stage), i, stage)
        dst = stages[stage].at[i].reshape(high, low, *mine.shape[-2:])
        return remote(
            view.at[:, 1 - value], dst, send_sem.at[i, stage + 1], recv_sem.at[i, stage + 1], (me ^ (1 << bit), core)
        )

    def small_copy(stage):
        device = partner if stage == bits else (me ^ (1 << stage), core)
        return remote(small_buf.at[stage], small_buf.at[bits + 1 + stage], small_send.at[stage], small_recv.at[stage], device)

    small_buf[0] = small_in[...]
    small_copy(0).start()

    def last_copy(i):
        return remote(out_buf(i), out_buf2(i), last_sem.at[0, i], last_sem.at[1, i], partner)

    out_own, out_other = scratch[-2], scratch[-1]

    def out_buf(i):
        return out_own.at[i]

    def out_buf2(i):
        return out_other.at[i]

    for tick in range(half + bits + 1):
        for stage in reversed(range(bits + 1)):
            i = tick - stage
            if not 0 <= i < half:
                continue
            if stage == 0:
                for c in range(2):

                    @pl.when(core == c)
                    def _(i=i, c=c):
                        fetch(i, c).wait()

                swap(i, 0).wait_recv()
                add_rows(mine.at[i], other.at[i], other.at[i])
            else:
                copy = stage_copy(i, stage - 1)
                copy.wait_recv()
                view, value, low, high, bit = split(source(i, stage - 1), i, stage - 1)
                dst = stages[stage - 1].at[i]
                if stage < bits:
                    kept = view.at[:, value]

                    def one(index, carry, kept=kept, dst=dst, low=low):
                        dst[index] = narrow(kept[index // low, index % low].astype(F32) + dst[index].astype(F32))
                        return carry

                    lax.fori_loop(0, high * low, one, 0)
                else:
                    total = view[0, value, 0].astype(F32) + dst[0].astype(F32)
                    out_own[i] = narrow(total)
                    for c in range(2):

                        @pl.when(core == c)
                        def _(i=i, c=c, total=total):
                            out[2 * i + c] = total

            if stage < bits:
                stage_copy(i, stage).start()
            else:
                last_copy(i).start()
        if 1 <= tick <= bits + 1:
            stage = tick - 1
            small_copy(stage).wait_recv()
            total = small_buf[stage] + small_buf[bits + 1 + stage]
            if stage < bits:
                small_buf[stage + 1] = total
                small_copy(stage + 1).start()
            else:
                small_out[...] = total
    for i in range(half):
        last_copy(i).wait_recv()
        for c in range(2):

            @pl.when(core == c)
            def _(i=i, c=c):
                out[2 * i + 1 - c] = out_other[i].astype(F32)

    for i in range(half):
        swap(i, 0).wait_send()
        for stage in range(bits):
            stage_copy(i, stage).wait_send()
        last_copy(i).wait_send()
    for stage in range(bits + 1):
        small_copy(stage).wait_send()


def reduce_all(n, parts, group, small):
    pieces = len(parts) + group.shape[1]
    half = pieces // 2
    _, rows, width = parts[0].shape
    bits = n.bit_length() - 1
    stage_shapes = [pltpu.VMEM((half, n >> (s + 1), rows, width), BF) for s in range(bits)]
    return pl.pallas_call(
        functools.partial(reduce_kernel, n, len(parts), group.shape[1]),
        out_shape=(jax.ShapeDtypeStruct((pieces, rows, width), F32), jax.ShapeDtypeStruct(small.shape, F32)),
        in_specs=[pl.BlockSpec(memory_space=pl.ANY)] * (len(parts) + 1) + [pl.BlockSpec(memory_space=pltpu.VMEM)],
        out_specs=(pl.BlockSpec(memory_space=pltpu.VMEM), pl.BlockSpec(memory_space=pltpu.VMEM)),
        scratch_shapes=[pltpu.VMEM((half, n, rows, width), BF), pltpu.VMEM((half, n, rows, width), BF)]
        + stage_shapes
        + [
            pltpu.SemaphoreType.DMA((half,)),
            pltpu.SemaphoreType.DMA((half, bits + 1)),
            pltpu.SemaphoreType.DMA((half, bits + 1)),
            pltpu.VMEM((2 * (bits + 1),) + small.shape, F32),
            pltpu.SemaphoreType.DMA((bits + 1,)),
            pltpu.SemaphoreType.DMA((bits + 1,)),
            pltpu.SemaphoreType.DMA((2, half)),
            pltpu.VMEM((half, rows, width), BF),
            pltpu.VMEM((half, rows, width), BF),
        ],
        compiler_params=pltpu.CompilerParams(collective_id=0, has_side_effects=True, vmem_limit_bytes=VMEM_LIMIT),
    )(*parts, group, small)


def whole(shape=None):
    return pl.BlockSpec(memory_space=pltpu.VMEM)


def call(kernel, outs, *args):
    return pl.pallas_call(
        kernel,
        out_shape=tuple(jax.ShapeDtypeStruct(shape, kind) for shape, kind in outs),
        in_specs=[whole()] * len(args),
        out_specs=tuple(whole() for _ in outs),
        compiler_params=pltpu.CompilerParams(vmem_limit_bytes=VMEM_LIMIT),
    )(*args)


def per_device(
    n, hidden, encodings, lengths, cotangent, wq, wk, wv, wo, wcq, wck, wcv, wco, w_in, w_out,
    gain_self, gain_cross, gain_feed, table,
):
    rows, width = hidden.shape[2], hidden.shape[3]
    slot = encodings.shape[3]
    passages = lengths.shape[2]
    units = w_in.shape[1]
    pairs = width // (2 * HD)
    keys = passages * slot
    own = hidden.reshape(rows, width)
    cot = cotangent.reshape(rows, width)
    g1, g2, g3 = (gain.reshape(1, width) for gain in (gain_self, gain_cross, gain_feed))
    length_row = lengths.reshape(passages)
    source = lax.all_to_all(encodings, "pass", split_axis=2, concat_axis=0, tiled=True).reshape(keys, width)

    sixteen, wide = ((rows, width), BF), ((rows, width), F32)
    h1, q, k, v, mix1, after_self, h2, cq = call(
        self_forward_kernel,
        [sixteen] * 5 + [wide, sixteen, sixteen],
        own, wq, wk, wv, wo, wcq, g1, g2, table,
    )

    block = 4 * slot
    steps = keys // block
    stats = jax.ShapeDtypeStruct((pairs, 2 * rows), F32)
    smem = pl.BlockSpec(memory_space=pltpu.SMEM)
    tile = pl.BlockSpec((block, width), lambda i: (i, 0))
    square = pl.BlockSpec((width, width), lambda i: (0, 0))
    query = pl.BlockSpec((rows, width), lambda i: (0, 0))
    stat = pl.BlockSpec((pairs, 2 * rows), lambda i: (0, 0))
    ck, cv, mix_t, lse = pl.pallas_call(
        functools.partial(cross_forward_kernel, slot),
        grid=(steps,),
        out_shape=(
            jax.ShapeDtypeStruct((keys, width), BF),
            jax.ShapeDtypeStruct((keys, width), BF),
            jax.ShapeDtypeStruct((width, rows), F32),
            stats,
        ),
        in_specs=[smem, tile, square, square, query],
        out_specs=(tile, tile, pl.BlockSpec((width, rows), lambda i: (0, 0)), stat),
        scratch_shapes=[
            pltpu.VMEM((pairs, 2 * rows, 2 * HD), BF),
            pltpu.VMEM((pairs, 2 * rows), F32),
            pltpu.VMEM((pairs, 2 * rows), F32),
            pltpu.VMEM((width, rows), F32),
        ],
        compiler_params=pltpu.CompilerParams(vmem_limit_bytes=VMEM_LIMIT),
    )(length_row, source, wck, wcv, cq)

    pieces = units // width
    result, grad_cross, gmix, delta, dg3, d_in, d_out, d_co = call(
        feed_kernel,
        [wide, wide, sixteen, ((pairs, 2 * rows), F32), ((1, width), F32), ((pieces, width, width), BF),
         ((units, width), BF), ((width, width), BF)],
        mix_t, after_self, cot, wco, w_in, w_out, g3,
    )

    enc_grad, dcq, d_ck, d_cv = pl.pallas_call(
        functools.partial(cross_backward_kernel, slot),
        grid=(steps,),
        out_shape=(
            jax.ShapeDtypeStruct((keys, width), BF),
            jax.ShapeDtypeStruct((rows, width), BF),
            jax.ShapeDtypeStruct((width, width), BF),
            jax.ShapeDtypeStruct((width, width), BF),
        ),
        in_specs=[smem, tile, tile, tile, square, square, query, query, stat, stat],
        out_specs=(tile, query, square, square),
        scratch_shapes=[
            pltpu.VMEM((pairs, 2 * rows, 2 * HD), BF),
            pltpu.VMEM((pairs, 2 * rows, 2 * HD), BF),
            pltpu.VMEM((width, rows), F32),
            pltpu.VMEM((block, 2 * width), BF),
            pltpu.VMEM((width, 2 * width), F32),
        ],
        compiler_params=pltpu.CompilerParams(vmem_limit_bytes=VMEM_LIMIT),
    )(length_row, source, ck, cv, wck, wcv, cq, gmix, lse, delta)
    returned = lax.all_to_all(
        enc_grad.reshape(passages, 1, 1, slot, width), "pass", split_axis=0, concat_axis=2, tiled=True
    )

    gain_kind = ((1, width), F32)
    squared = ((width, width), BF)
    hidden_grad, d_cq, d_so, d_q, d_k, d_v, dg1, dg2, dtable = call(
        self_backward_kernel,
        [wide] + [squared] * 5 + [gain_kind, gain_kind, (table.shape, F32)],
        own, h1, q, k, v, mix1, after_self, h2, dcq, grad_cross, wq, wk, wv, wo, wcq, g1, g2, table,
    )

    share = width // n
    if n & (n - 1) == 0 and share % 16 == 0:
        squares = [d_q, d_k, d_v, d_so, d_cq, d_ck, d_cv, d_co]
        parts = [d.reshape(n, share, width) for d in squares]
        parts += [d_in[i].reshape(n, share, width) for i in range(pieces)]
        big = d_out.reshape(n, pieces, share, width)
        flat = jnp.concatenate([dg1, dg2, dg3, jnp.pad(dtable.reshape(1, -1), ((0, 0), (0, width - dtable.size))),
                                jnp.zeros((4, width), F32)], axis=0)
        sums, small = reduce_all(n, parts, big, flat)
        totals = [sums[i] for i in range(8)]
        count = len(squares)
        in_total = jnp.concatenate([sums[count + i] for i in range(pieces)], axis=1)
        out_total = sums[count + pieces :].reshape(pieces * share, width)
        me = lax.axis_index("pass")
        gains = [lax.dynamic_slice(small[i], (me * share,), (share,)) for i in range(3)]
        table_sum = small[3, : dtable.size].reshape(table.shape)
    else:
        both = [d_q, d_k, d_v, d_so, d_cq, d_ck, d_cv, d_co, d_in.transpose(1, 0, 2).reshape(width, units), d_out]

        def total(part):
            shared = lax.psum_scatter(part, "pass", scatter_dimension=0, tiled=True)
            return lax.psum(shared.astype(BF), "pb").astype(F32)

        sums = [total(part.astype(F32)) for part in both]
        totals, in_total, out_total = sums[:8], sums[8], sums[9]
        gains = [total(part.reshape(width)) for part in (dg1, dg2, dg3)]
        table_sum = lax.psum(dtable, ("pass", "pb"))
    return (
        (result.reshape(hidden.shape), hidden_grad.reshape(hidden.shape), returned)
        + tuple(totals)
        + (in_total, out_total)
        + tuple(gains)
        + (table_sum,)
    )


def solution(mesh):
    rows = P("pb", "pass", None, None)
    passage = P("pass", "pb", None, None, None)
    in_specs = (rows, passage, P("pb", "pass", None), rows) + (P(),) * 14
    out_specs = (rows, rows, passage) + (P("pass", None),) * 10 + (P("pass"),) * 3 + (P(),)
    return jax.shard_map(
        functools.partial(per_device, mesh.shape["pass"]),
        mesh=mesh,
        in_specs=in_specs,
        out_specs=out_specs,
        check_vma=False,
    )
```

time: 1890 us -> 378 us (0.20)
  waiting for transfers between devices: 1280 us -> 62.4 us
  matrix products: 343 us -> 0 us
  Pallas kernels: 0 us -> 281 us
  blocking collectives: 116 us -> 0 us
  local copies, waits for them, and re-layouts: 70.7 us -> 20.5 us
  other arithmetic: 41.4 us -> 0.85 us
    reduce_scatter x8 -> x0, waiting for transfers between devices: 992 us -> none  [the longest x1 175 us: per_device(): lax.psum_scatter(grad_feed_out, 'pass', scatter_dimension=0, tiled=True)]
    dot_general x200 -> x0, matrix products: 343 us -> none  [the longest x82 121 us: product_nt(): lax.dot_general(left, right, (((1,), (1,)), ((), ())), preferred_element_...]
    pallas_call x0 -> x6, Pallas kernels: none -> 281 us  [the longest x1 206 us: reduce_all(): pl.pallas_call(functools.partial(reduce_kernel, n, len(parts), group.shap...]
    unnamed x13 -> x0, waiting for transfers between devices: 263 us -> none
    psum x2 -> x0, blocking collectives: 64.4 us -> none  [the longest x1 47 us: per_device(): table_sum = lax.psum(grad_table, ('pass', 'pb'))]
    unnamed x1 -> x0, blocking collectives: 51.7 us -> none
    all_to_all x1, waiting for transfers between devices: 23.8 us -> 62.4 us  [per_device(): lax.all_to_all(encodings, 'pass', split_axis=2, concat_axis=0, tiled=True)]
    dynamic_update_slice x12 -> x0, local copies, waits for them, and re-layouts: 35.2 us -> none  [one_head(): lax.dynamic_update_index_in_dim(kept_scores, grad_scores, index, 0)]
  transfers between devices with their start and end apart: 13 -> 2, of which waited for: 10 -> 1; matrix products, arithmetic and copies ran while one was open for 13% -> 5% of each run, Pallas kernels for 0% -> 59%
where the time goes in v1:
time: 378 us; the launch traced here: 377 us
  Pallas kernels  281 us (74%)
  waiting for transfers between devices  62.4 us (17%)
  local copies, waits for them, and re-layouts  20.5 us (5%)
  starting transfers between devices  11.7 us (3%)
    pallas_call x1, Pallas kernels, reduce_all(): pl.pallas_call(functools.partial(reduce_kernel, n, len(parts), group.shap...  206 us
    all_to_all x1, waiting for transfers between devices, per_device(): lax.all_to_all(encodings, 'pass', split_axis=2, concat_axis=0, tiled=True)  62.4 us
    pallas_call x3, Pallas kernels, call(): pl.pallas_call(kernel, out_shape=tuple((jax.ShapeDtypeStruct(shape, kind)...  31.4 us
    pallas_call x1, Pallas kernels, per_device(): pl.pallas_call(functools.partial(cross_backward_kernel, slot), grid=(step...  25.2 us
    pallas_call x1, Pallas kernels, per_device(): pl.pallas_call(functools.partial(cross_forward_kernel, slot), grid=(steps...  18.9 us
  transfers between devices with their start and end apart: 2, of which 1 were waited for; matrix products, arithmetic and copies ran while one was open for 5% of the time, Pallas kernels for 59%

profile of v1, /device:TPU:13, one launch (start us, length us, event | category | flops | bytes accessed | tf_op | source)
XLA Modules:
  0.0 377.3 jit_solution(10399988494619451166)
XLA Ops:
  0.7 0.0 copy-start.2
  0.7 0.0 copy-start.3
  0.7 0.0 copy-start.1
  0.7 0.0 copy-start.4
  0.7 6.8 %all-to-all-start = ((bf16[1,1,16,128,768]{4,3,1,0,2:T(8,128)(2,1)}), bf16[1,1,16,128,768]{4,3,1,0,2:T(8,128)(2,1)S(1)}, u32[]{:S(2)}, u32[]{:S(2)}) async-start(bf16[1,1,16,128,768]{4,3,1,0,2:T(8,128)(2,1)} %bitcast.63), calls=%async_computation | async-start | bytes 6291456 | tf_op jit(solution)/shard_map/all_to_all | solution.py:533
  7.5 0.6 reshape.110.g1
  8.0 0.6 reshape.111.g2
  8.6 0.7 copy.42.table
  9.3 0.6 reshape.113.g3
  9.9 5.4 %shard_map.305 = (bf16[128,768]{1,0:T(8,128)(2,1)}, bf16[128,768]{1,0:T(8,128)(2,1)}, bf16[128,768]{1,0:T(8,128)(2,1)}, bf16[128,768]{1,0:T(8,128)(2,1)}, bf16[1...) custom-call(bf16[128,768]{1,0:T(8,128)(2,1)} %bitcast.73, ...), custom_call_target="tpu_custom_call" | custom-call | tf_op jit(solution)/shard_map/pallas_call | solution.py:510
  15.3 62.4 %all-to-all-done = bf16[1,1,16,128,768]{4,3,1,0,2:T(8,128)(2,1)S(1)} async-done(((bf16[1,1,16,128,768]{4,3,1,0,2:T(8,128)(2,1)}), bf16[1,1,16,128,768]{4,3,1,0,2:T(8,128)(2,1)S(1)}, u32[]{:S(2)}, u32[]{:S(2)}) %all-to-all-start) | async-done | bytes 3145760 | tf_op jit(solution)/shard_map/all_to_all | solution.py:533
  77.7 1.7 copy-done
  79.3 18.9 %shard_map.306 = (bf16[2048,768]{1,0:T(8,128)(2,1)}, bf16[2048,768]{1,0:T(8,128)(2,1)}, f32[768,128]{1,0:T(8,128)}, f32[6,256]{1,0:T(8,128)}) custom-call(s32[16]{0:T(128)} %bitcast.77, bf16[2048,768]{1,0:T(8,128)(2,1)} %bitcast.55, bf16[768,768]{1,0:T(8,128)(2,1)} %wk.6, bf16[768,768]{1,0:T(8,128)(2,1)} %wv.6, bf16[128,768]{1,0:T(8,128)(2,1)} %get-tuple-element.52.cq), custom_call_target="tpu_custom_call" | custom-call | tf_op jit(solution)/shard_map/pallas_call | solution.py:550
  98.2 14.5 %shard_map.307 = (f32[128,768]{1,0:T(8,128)}, f32[128,768]{1,0:T(8,128)}, bf16[128,768]{1,0:T(8,128)(2,1)}, f32[6,256]{1,0:T(8,128)}, f32[1,768]{1,0:T(1,128)}, ...) custom-call(f32[768,128]{1,0:T(8,128)} %get-tuple-element.53.mix_t, ...), custom_call_target="tpu_custom_call" | custom-call | tf_op jit(solution)/shard_map/pallas_call | solution.py:510
  112.8 25.2 %shard_map.308 = (bf16[2048,768]{1,0:T(8,128)(2,1)}, bf16[128,768]{1,0:T(8,128)(2,1)}, bf16[768,768]{1,0:T(8,128)(2,1)}, bf16[768,768]{1,0:T(8,128)(2,1)}) custom-call(s32[16]{0:T(128)} %bitcast.78, bf16[2048,768]{1,0:T(8,128)(2,1)} %bitcast.56, bf16[2048,768]{1,0:T(8,128)(2,1)} %get-tuple-element.62.k, bf16[2048,768]{1,0:T(8,128)(2,1)} %get-tuple-element.63.v, ...), custom_call_target="tpu_custom_call" | custom-call | tf_op jit(solution)/shard_map/pallas_call | solution.py:578
  138.0 4.9 %all-to-all-start.1 = ((bf16[16,1,1,128,768]{4,3,2,1,0:T(8,128)(2,1)}), bf16[16,1,1,128,768]{4,3,2,1,0:T(8,128)(2,1)S(1)}, u32[]{:S(2)}, u32[]{:S(2)}) async-start(bf16[16,1,1,128,768]{4,3,2,1,0:T(8,128)(2,1)} %bitcast.64), calls=%async_computation.1 | async-start | bytes 6291456 | tf_op jit(solution)/shard_map/all_to_all | solution.py:598
  142.9 11.4 %shard_map.309 = (f32[128,768]{1,0:T(8,128)}, bf16[768,768]{1,0:T(8,128)(2,1)}, bf16[768,768]{1,0:T(8,128)(2,1)}, bf16[768,768]{1,0:T(8,128)(2,1)}, bf16[768,768...) custom-call(bf16[128,768]{1,0:T(8,128)(2,1)} %bitcast.74, ...), custom_call_target="tpu_custom_call" | custom-call | tf_op jit(solution)/shard_map/pallas_call | solution.py:510
  154.3 0.8 reshape.126
  155.2 1.3 concatenate.6.refs_13_
  156.5 4.6 %fusion.3 = (bf16[1,768,768]{2,1,0:T(8,128)(2,1)}, bf16[1,768,768]{2,1,0:T(8,128)(2,1)}, bf16[1,768,768]{2,1,0:T(8,128)(2,1)}, bf16[1,768,768]{2,1,0:T(8,128)(2,1)}) fusion(bf16[4,768,768]{2,1,0:T(8,128)(2,1)} %get-tuple-element.79), kind=kLoop, calls=%fused_computation.20 | loop fusion | bytes 9437184 | tf_op jit(solution)/shard_map/slice | solution.py:614
  161.2 205.7 %shard_map.310 = (f32[16,48,768]{2,1,0:T(8,128)}, f32[8,768]{1,0:T(8,128)}) custom-call(bf16[16,48,768]{2,1,0:T(8,128)(2,1)} %bitcast.70, bf16[16,48,768]{2,1,0:T(8,128)(2,1)} %bitcast.71, bf16[16,48,768]{2,1,0:T(8,128)(2,1)} %bitcast.72, bf16[16,48,768]{2,1,0:T(8,128)(2,1)} %bitcast.69, bf16[16,48,768]{2,1,0:T(8,128)(2,1)} %bitcast.68, ...), custom_call_target="tpu_custom_call" | custom-call | tf_op jit(solution)/shard_map/pallas_call | solution.py:483
  366.8 1.9 slice.79
  368.7 0.7 slice_reduce_fusion
  369.5 0.1 reshape_squeeze.19
  369.6 0.7 copy.45
  370.2 0.9 fusion.4
  371.1 0.6 fusion.2
  371.7 0.6 fusion
  372.3 2.5 slice_bitcast_fusion.3
  374.8 0.9 pad_maximum_fusion
  375.7 0.0 all-to-all-done.1
  375.7 1.7 copy.47
  (9 shorter events, 0.0 us)
Async XLA Ops:
  0.7 6.8 %copy-start.2 = (f32[768]{0:T(1024)S(1)}, f32[768]{0:T(1024)}, u32[]{:S(2)}) copy-start(f32[768]{0:T(1024)} %param.32) | copy-start | bytes 9220
  0.7 7.4 %copy-start.3 = (f32[768]{0:T(1024)S(1)}, f32[768]{0:T(1024)}, u32[]{:S(2)}) copy-start(f32[768]{0:T(1024)} %param.33) | copy-start | bytes 9220
  0.7 7.9 %copy-start.1 = (f32[32,12]{0,1:T(8,128)S(1)}, f32[32,12]{0,1:T(8,128)}, u32[]{:S(2)}) copy-start(f32[32,12]{0,1:T(8,128)} %param.35) | copy-start | bytes 4612
  0.7 8.6 %copy-start.4 = (f32[768]{0:T(1024)S(1)}, f32[768]{0:T(1024)}, u32[]{:S(2)}) copy-start(f32[768]{0:T(1024)} %param.34) | copy-start | bytes 9220
  0.7 77.0 %all-to-all-start = ((bf16[1,1,16,128,768]{4,3,1,0,2:T(8,128)(2,1)}), bf16[1,1,16,128,768]{4,3,1,0,2:T(8,128)(2,1)S(1)}, u32[]{:S(2)}, u32[]{:S(2)}) async-start(bf16[1,1,16,128,768]{4,3,1,0,2:T(8,128)(2,1)} %bitcast.63), calls=%async_computation | async-start | bytes 6291456 | tf_op jit(solution)/shard_map/all_to_all | solution.py:533
  77.7 1.7 copy-start
  138.0 237.7 %all-to-all-start.1 = ((bf16[16,1,1,128,768]{4,3,2,1,0:T(8,128)(2,1)}), bf16[16,1,1,128,768]{4,3,2,1,0:T(8,128)(2,1)S(1)}, u32[]{:S(2)}, u32[]{:S(2)}) async-start(bf16[16,1,1,128,768]{4,3,2,1,0:T(8,128)(2,1)} %bitcast.64), calls=%async_computation.1 | async-start | bytes 6291456 | tf_op jit(solution)/shard_map/all_to_all | solution.py:598
  142.9 12.3 %copy-start.5 = (f32[1,768]{1,0:T(1,128)S(1)}, f32[1,768]{1,0:T(1,128)}, u32[]{:S(2)}) copy-start(f32[1,768]{1,0:T(1,128)} %get-tuple-element.83) | copy-start | bytes 9220

commit v2 on v1

--- a/solution.py
+++ b/solution.py
@@ -17,6 +17,7 @@
 MESH = pl.DeviceIdType.MESH
 ROOT = 0.7978845608028654
 VMEM_LIMIT = 56 << 20
+LAYER_LIMIT = 63 << 20
 
 
 def narrow(value):
@@ -72,9 +73,9 @@
 
 
 def head_bias(table, rows):
-    onehot = bucket_onehot_rows(table.shape[0], rows)
+    onehot = bucket_onehot_rows(table.shape[1], rows)
     return lax.dot_general(
-        table, onehot, (((0,), (0,)), ((), ())), precision=lax.Precision.HIGHEST,
+        table, onehot, (((1,), (0,)), ((), ())), precision=lax.Precision.HIGHEST,
         preferred_element_type=F32,
     )
 
@@ -117,7 +118,7 @@
     q_out[...] = q
     k_out[...] = k
     v_out[...] = v
-    bias = head_bias(table[...], rows)
+    bias = head_bias(table[...].T, rows)
     allowed = causal_mask(rows)
     mixed = []
     for pair in range(pairs):
@@ -278,7 +279,7 @@
     sb = narrow(grad)
     d_o[...] = narrow(dot_tn(mix[...], sb))
     gmix = narrow(dot_nt(sb, wo[...]))
-    bias = head_bias(table[...], rows)
+    bias = head_bias(table[...].T, rows)
     allowed = causal_mask(rows)
     dq_parts, dk_parts, dv_parts, sums = [], [], [], []
     for pair in range(pairs):
@@ -502,6 +503,695 @@
     )(*parts, group, small)
 
 
+def halving_order(bits, piece):
+    first = list(range(bits))
+    if piece % 2 and bits > 1:
+        first[0], first[1] = first[1], first[0]
+    return first
+
+
+def drain_order(bits, early, pieces):
+    free, waiting, steps, now = {0: 5.0, 1: 5.0, 2: 13.0}, [], [], 0.0
+
+    def send(piece, stage, time):
+        bit = halving_order(bits, piece)[stage]
+        link = min(bit, 2)
+        free[link] = max(time, free.get(link, 0.0)) + 1.0 / (1 << stage) + (0.1 if bit > 2 else 0.0)
+        waiting.append((free[link] + 0.3, piece, stage))
+
+    for piece in range(early):
+        send(piece, 0, 0.0)
+    first = early
+    while waiting:
+        waiting.sort()
+        time, piece, stage = waiting.pop(0)
+        now = max(now, time)
+        steps.append(("arrive", piece, stage))
+        if stage + 1 < bits:
+            send(piece, stage + 1, now)
+        first -= stage == 0
+        if first == 0:
+            first = pieces
+            for piece in range(early, pieces):
+                steps.append(("begin", piece, 0))
+                send(piece, 0, now)
+    for turn in range(bits):
+        steps.insert((turn + 1) * len(steps) // (bits + 1), ("small", 0, 0))
+    return steps
+
+
+INPUTS = (
+    "lengths", "encodings", "wq", "wk", "wv", "wo", "wcq", "wck", "wcv", "wco", "w_in", "w_out",
+    "hidden", "cot", "g1", "g2", "g3", "table",
+)
+OUTPUTS = (
+    "result_out", "hidden_out", "enc_out", "sq", "sk", "sv", "so", "cqo", "cko", "cvo", "coo", "fin", "fout",
+    "gs", "gc", "gf", "table_out",
+)
+SCRATCH = (
+    "L1", "L2", "R", "give", "own_late", "send_late", "encb", "kb", "vb", "eg", "wb", "masked", "gmasked", "dq_t",
+    "q", "k", "v", "after_self", "grad_cross", "top", "lse", "delta", "swap_send", "swap_recv", "mine",
+)
+AFTER = (
+    "last_own", "last_other", "small_g", "small_t", "load_sem", "pair_send", "pair_recv", "rs_send", "rs_recv",
+    "in_send", "in_recv", "a2a_send", "a2a_recv", "a2a_own", "small_send", "small_recv", "last_send", "last_recv",
+)
+SQUARES = ("wq", "wk", "wv", "wo", "wcq", "wck", "wcv", "wco")
+
+
+def layer_kernel(n, slot, count_in, count_out, *refs):
+    bits = n.bit_length() - 1
+    names = INPUTS + OUTPUTS + SCRATCH + tuple("s%d" % b for b in range(bits)) + AFTER
+    r = dict(zip(names, refs, strict=True))
+    lengths, table, hidden = r["lengths"], r["table"], r["hidden"]
+    stages = [r["s%d" % b] for b in range(bits)]
+    mine, wb, L1, L2 = r["mine"], r["wb"], r["L1"], r["L2"]
+    pieces, _, share, half = mine.shape
+    rows, width = hidden.shape
+    units = count_out * width
+    span = count_in * half
+    pairs = width // (2 * HD)
+    two = 2 * HD
+    me, core = lax.axis_index("pass"), lax.axis_index("pb")
+    partner = (me, 1 - core)
+    gains = {name: r[name][...].reshape(1, width) for name in ("g1", "g2", "g3")}
+    W = {name: wb.at[i] for i, name in enumerate(SQUARES)}
+
+    def remote(src, dst, send, recv, device):
+        return pltpu.make_async_remote_copy(
+            src_ref=src, dst_ref=dst, send_sem=send, recv_sem=recv, device_id=device, device_id_type=MESH
+        )
+
+    parts = units // half
+    loads = [(r[w], wb.at[i]) for i, w in enumerate(SQUARES)]
+    tiles = [mine.at[i].reshape(width, half) for i in range(2 * parts)]
+    for j in range(parts):
+        loads.append((r["w_in"].at[:, j * half : (j + 1) * half], tiles[j]))
+        for c in range(2):
+            loads.append((
+                r["w_out"].at[j * half : (j + 1) * half, c * half : (c + 1) * half],
+                tiles[parts + j].at[c * half : (c + 1) * half],
+            ))
+
+    def load(i):
+        return pltpu.make_async_copy(loads[i][0], loads[i][1], r["load_sem"].at[i])
+
+    for i in range(len(SQUARES)):
+        load(i).start()
+
+    barrier = pltpu.get_barrier_semaphore()
+    pl.semaphore_signal(barrier, inc=1, device_id=partner, device_id_type=MESH)
+
+    def greet(d, carry):
+        pl.semaphore_signal(barrier, inc=1, device_id=(me ^ d, core), device_id_type=MESH)
+        return carry
+
+    lax.fori_loop(1, n, greet, 0)
+    pl.semaphore_wait(barrier, n)
+
+    def passage_at(p):
+        return pl.ds(pl.multiple_of(p * slot, slot), slot)
+
+    def bring(q):
+        return remote(r["encodings"].at[q], r["encb"].at[passage_at(me)], r["in_send"].at[q], r["in_recv"].at[me], (q, core))
+
+    def arrived(p):
+        return remote(r["encodings"].at[p], r["encb"].at[passage_at(p)], r["in_send"].at[p], r["in_recv"].at[p], (p, core))
+
+    def bring_one(i, carry):
+        bring(me ^ (n // 2 + i)).start()
+        return carry
+
+    lax.fori_loop(0, n // 2, bring_one, 0)
+    quarter = n // 4
+
+    def bring_near(i, carry):
+        bring(me ^ (quarter + i)).start()
+        return carry
+
+    lax.fori_loop(0, quarter, bring_near, 0)
+
+    def bring_rest(i, carry):
+        bring(me ^ i).start()
+        return carry
+
+    lax.fori_loop(1, quarter, bring_rest, 0)
+    own_passage = pltpu.make_async_copy(r["encodings"].at[me], r["encb"].at[passage_at(me)], r["a2a_own"].at[0])
+    own_passage.start()
+    for i in range(len(SQUARES), len(loads)):
+        load(i).start()
+
+    value = hidden[...].astype(F32)
+    h1 = narrow(rms(value, gains["g1"]))
+    L1[0, :, :width] = h1
+    for i, name in enumerate(("q", "k", "v")):
+        load(i).wait()
+        r[name][...] = narrow(dot_nn(h1, wb[i]))
+    bias = head_bias(table[...], rows)
+    allowed = causal_mask(rows)
+
+    def self_chances(pair):
+        at = slice(pair * two, (pair + 1) * two)
+        masked = pair_mask(r["q"][:, at])
+        scores = dot_nt(r["k"][:, at], masked)
+        both = jnp.concatenate([toeplitz(bias[2 * pair + i : 2 * pair + i + 1], rows) for i in range(2)], axis=1)
+        scores = jnp.where(allowed, scores + both, NEG)
+        raised = jnp.exp(scores - jnp.max(scores, axis=0, keepdims=True))
+        return at, masked, raised / jnp.sum(raised, axis=0, keepdims=True)
+
+    for pair in range(pairs):
+        at, _, chances = self_chances(pair)
+        r["dq_t"][at, :] = pair_diag(dot_tn(r["v"][:, at], narrow(chances)), rows)
+    mix1 = narrow(r["dq_t"][...].T)
+    L1[0, :, 2 * width :] = mix1
+    load(3).wait()
+    after_self = value + dot_nn(mix1, W["wo"][...])
+    r["after_self"][...] = after_self
+    h2 = narrow(rms(after_self, gains["g2"]))
+    L1[0, :, width : 2 * width] = h2
+    load(4).wait()
+    cq = narrow(dot_nn(h2, W["wcq"][...]))
+    for pair in range(pairs):
+        r["masked"][pair] = pair_mask(cq[:, pair * two : (pair + 1) * two])
+    r["top"][...] = jnp.full(r["top"].shape, NEG, F32)
+    r["lse"][...] = jnp.zeros(r["lse"].shape, F32)
+    r["dq_t"][...] = jnp.zeros(r["dq_t"].shape, F32)
+
+    def pair_copy(i):
+        src = (L1.at[0], L2.at[0], r["give"])[i]
+        dst = (L1, L2, r["R"])[i].at[1]
+        return remote(src, dst, r["pair_send"].at[i], r["pair_recv"].at[i], partner)
+
+    pair_copy(0).start()
+
+    place = lax.broadcasted_iota(jnp.int32, (slot, 2 * rows), 0)
+
+    def spread(row):
+        return jnp.concatenate(
+            [jnp.broadcast_to(row[:, :rows], (HD, rows)), jnp.broadcast_to(row[:, rows:], (HD, rows))], axis=0
+        )
+
+    load(5).wait()
+    load(6).wait()
+    own_passage.wait()
+    few = 2
+
+    def forward_block(turn, carry):
+        first = (turn ^ (me // few)) * few
+        for i in range(few):
+
+            @pl.when(first + i != me)
+            def _(i=i):
+                arrived(first + i).wait_recv()
+
+        at = pl.ds(pl.multiple_of(first * slot, few * slot), few * slot)
+        source = r["encb"][at]
+        r["kb"][at] = narrow(dot_nn(source, W["wck"][...]))
+        r["vb"][at] = narrow(dot_nn(source, W["wcv"][...]))
+        valid = jnp.concatenate([place < lengths[first + i] for i in range(few)], axis=0)
+        for pair in range(pairs):
+            cols = slice(pair * two, (pair + 1) * two)
+            scores = jnp.where(valid, dot_nt(r["kb"][at, cols], r["masked"][pair]), NEG)
+            before = r["top"][pair : pair + 1]
+            now = jnp.maximum(before, jnp.max(scores, axis=0, keepdims=True))
+            r["top"][pair : pair + 1] = now
+            fade = jnp.exp(before - now)
+            raised = jnp.exp(scores - now)
+            r["lse"][pair : pair + 1] = r["lse"][pair : pair + 1] * fade + jnp.sum(raised, axis=0, keepdims=True)
+            part = pair_diag(dot_tn(r["vb"][at, cols], narrow(raised)), rows)
+            r["dq_t"][cols, :] = r["dq_t"][cols, :] * spread(fade) + part
+        return carry
+
+    lax.fori_loop(0, n // few, forward_block, 0)
+    for pair in range(pairs):
+        cols = slice(pair * two, (pair + 1) * two)
+        sums = r["lse"][pair : pair + 1]
+        r["lse"][pair : pair + 1] = r["top"][pair : pair + 1] + jnp.log(sums)
+        r["dq_t"][cols, :] = r["dq_t"][cols, :] * spread(1.0 / sums)
+
+    mix2 = narrow(r["dq_t"][...].T)
+    L2[0, :, units + width :] = mix2
+    load(7).wait()
+    after_cross = r["after_self"][...] + dot_nn(mix2, W["wco"][...])
+    h3 = narrow(rms(after_cross, gains["g3"]))
+    L2[0, :, units : units + width] = h3
+    cb = r["cot"][...]
+    outs = [after_cross[:, c * half : (c + 1) * half] for c in range(2)]
+    into = jnp.zeros((rows, width), F32)
+    for j in range(parts):
+        for i in range(3):
+            load(len(SQUARES) + 3 * j + i).wait()
+        inner = dot_nn(h3, tiles[j][...])
+        bent = jnp.tanh(ROOT * (inner + 0.044715 * (inner * inner * inner)))
+        active = narrow(0.5 * inner * (1.0 + bent))
+        L2[0, :, j * half : (j + 1) * half] = active
+        slope = 0.5 * (1.0 + bent) + (0.5 * ROOT) * inner * (1.0 - bent * bent) * (1.0 + (3 * 0.044715) * inner * inner)
+        back = jnp.zeros((rows, half), F32)
+        for c in range(2):
+            tile = tiles[parts + j][c * half : (c + 1) * half]
+            outs[c] = outs[c] + dot_nn(active, tile)
+            back = back + dot_nt(cb[:, c * half : (c + 1) * half], tile)
+        gi = narrow(back * slope)
+        to = j % count_in
+        c = j // count_in
+
+        @pl.when(core == c)
+        def _(gi=gi, to=to):
+            r["R"][0, :, to * half : (to + 1) * half] = gi
+
+        @pl.when(core != c)
+        def _(gi=gi, to=to):
+            r["give"][:, to * half : (to + 1) * half] = gi
+
+        into = into + dot_nt(gi, tiles[j][...])
+    pair_copy(1).start()
+    for c in range(2):
+        r["result_out"][:, c * half : (c + 1) * half] = outs[c]
+    back, dg3 = rms_back(after_cross, gains["g3"], into)
+    grad = cb.astype(F32) + back
+    r["grad_cross"][...] = grad
+    gb = narrow(grad)
+    for c in range(2):
+        for j, value in enumerate((cb, gb)):
+            part = value[:, c * half : (c + 1) * half]
+
+            @pl.when(core == c)
+            def _(part=part, j=j):
+                r["R"][0, :, span + j * half : span + (j + 1) * half] = part
+
+            @pl.when(core != c)
+            def _(part=part, j=j):
+                r["give"][:, span + j * half : span + (j + 1) * half] = part
+
+    pair_copy(2).start()
+    gmix = narrow(dot_nt(gb, W["wco"][...]))
+    product = gmix.astype(F32).T * r["dq_t"][...]
+    for pair in range(pairs):
+        at = slice(pair * two, (pair + 1) * two)
+        r["gmasked"][pair] = pair_mask(gmix[:, at])
+        part = product[at]
+        r["delta"][pair : pair + 1] = jnp.concatenate(
+            [jnp.sum(part[:HD], axis=0, keepdims=True), jnp.sum(part[HD:], axis=0, keepdims=True)], axis=1
+        )
+    r["dq_t"][...] = jnp.zeros(r["dq_t"].shape, F32)
+    group = 4
+    blocks = n // group
+    block = group * slot
+
+    def send_back(passage, wait):
+        at = passage_at(passage)
+        away = remote(r["eg"].at[at], r["enc_out"].at[me], r["a2a_send"].at[passage], r["a2a_recv"].at[me], (passage, core))
+        stay = pltpu.make_async_copy(r["eg"].at[at], r["enc_out"].at[me], r["a2a_own"].at[0])
+
+        @pl.when(passage != me)
+        def _():
+            away.wait_send() if wait else away.start()
+
+        @pl.when(passage == me)
+        def _():
+            stay.wait() if wait else stay.start()
+
+    def cross_block(turn, carry):
+        first = (blocks - 1 - turn) ^ (me // group)
+        at = pl.ds(pl.multiple_of(first * block, block), block)
+        valid = jnp.concatenate([place < lengths[first * group + i] for i in range(group)], axis=0)
+        for pair in range(pairs):
+            cols = slice(pair * two, (pair + 1) * two)
+            key, value = r["kb"][at, cols], r["vb"][at, cols]
+            scores = jnp.where(valid, dot_nt(key, r["masked"][pair]), NEG)
+            chances = jnp.exp(scores - r["lse"][pair : pair + 1])
+            ds = narrow(chances * (dot_nt(value, r["gmasked"][pair]) - r["delta"][pair : pair + 1]))
+            r["vb"][at, cols] = narrow(dot_nn(narrow(chances), r["gmasked"][pair]))
+            r["dq_t"][cols, :] = r["dq_t"][cols, :] + pair_diag(dot_tn(key, ds), rows)
+            r["kb"][at, cols] = narrow(dot_nn(ds, r["masked"][pair]))
+        r["eg"][at] = narrow(dot_nt(r["kb"][at], W["wck"][...]) + dot_nt(r["vb"][at], W["wcv"][...]))
+        for i in range(group):
+            send_back(first * group + i, False)
+        return carry
+
+    def split(ref, piece, stage):
+        done = halving_order(bits, piece)[:stage]
+        bit = halving_order(bits, piece)[stage]
+        low = 1 << len([b for b in range(bit) if b not in done])
+        high = (n >> stage) // (2 * low)
+        return ref.reshape(high, 2, low, share, half), (me >> bit) & 1, low, high, bit
+
+    def source(piece, stage):
+        return mine.at[piece] if stage == 0 else stages[stage - 1].at[piece]
+
+    def stage_copy(piece, stage):
+        view, value, low, high, bit = split(source(piece, stage), piece, stage)
+        dst = stages[stage].at[piece].reshape(high, low, share, half)
+        sems = r["rs_send"].at[piece, stage], r["rs_recv"].at[piece, stage]
+        return remote(view.at[:, 1 - value], dst, *sems, (me ^ (1 << bit), core))
+
+    squares = ("sq", "sk", "sv", "so", "cqo", "cko", "cvo", "coo")
+    order = ["in"] * count_in + ["out"] * count_out + ["coo", "cko", "cvo", "cqo", "so", "sq", "sk", "sv"]
+    index = {name: order.index(name) for name in squares}
+
+    def put(piece, c, total):
+        name = order[piece]
+        if name == "in":
+            r["fin"][:, c * count_in * half + piece * half : c * count_in * half + (piece + 1) * half] = total
+        elif name == "out":
+            k = piece - count_in
+            r["fout"][k * share : (k + 1) * share, c * half : (c + 1) * half] = total
+        else:
+            r[name][:, c * half : (c + 1) * half] = total
+
+    def last_copy(piece):
+        sems = r["last_send"].at[piece], r["last_recv"].at[piece]
+        return remote(r["last_own"].at[piece], r["last_other"].at[piece], *sems, partner)
+
+    def arrive(piece, stage):
+        stage_copy(piece, stage).wait_recv()
+        view, value, low, high, bit = split(source(piece, stage), piece, stage)
+        kept = view.at[:, value]
+        dst = stages[stage].at[piece]
+        if stage + 1 < bits:
+
+            def one(i, carry):
+                dst[i] = narrow(kept[i // low, i % low].astype(F32) + dst[i].astype(F32))
+                return carry
+
+            lax.fori_loop(0, high * low, one, 0)
+            stage_copy(piece, stage + 1).start()
+        else:
+            total = kept[0, 0].astype(F32) + dst[0].astype(F32)
+            r["last_own"][piece] = narrow(total)
+            last_copy(piece).start()
+            for c in range(2):
+
+                @pl.when(core == c)
+                def _(c=c):
+                    put(piece, c, total)
+
+    def begin(piece):
+        stage_copy(piece, 0).start()
+
+    lax.fori_loop(0, blocks, cross_block, 0)
+
+    for i in range(3):
+        pair_copy(i).wait_recv()
+    F1, F2, FR = (r[x].reshape(2 * rows, r[x].shape[2]) for x in ("L1", "L2", "R"))
+
+    def owners(value):
+        return narrow(value).reshape(n, share, half)
+
+    for piece in range(count_in):
+        mine[piece] = owners(dot_tn(F2[:, units : units + width], FR[:, piece * half : (piece + 1) * half]))
+        begin(piece)
+    per = width // (count_out * share)
+    for part in range(count_out):
+        value = narrow(dot_tn(F2[:, part * width : (part + 1) * width], FR[:, span : span + half]))
+        value = value.reshape(per, count_out, share, half)
+        for k in range(count_out):
+            mine[count_in + k, part * per : (part + 1) * per] = value[:, k]
+    for k in range(count_out):
+        begin(count_in + k)
+    mine[index["coo"]] = owners(dot_tn(F2[:, units + width :], FR[:, span + half :]))
+    begin(index["coo"])
+
+    late_names = ("cqo", "so", "sq", "sk", "sv")
+    lefts = {"cqo": width, "so": 2 * width, "sq": 0, "sk": 0, "sv": 0}
+
+    def late_copy(i):
+        return remote(
+            r["send_late"].at[i], r["own_late"].at[i, 1], r["pair_send"].at[3 + i], r["pair_recv"].at[3 + i], partner
+        )
+
+    def late_give(name, value):
+        i = late_names.index(name)
+        for c in range(2):
+
+            @pl.when(core == c)
+            def _(c=c):
+                r["own_late"][i, 0] = value[:, c * half : (c + 1) * half]
+                r["send_late"][i] = value[:, (1 - c) * half : (2 - c) * half]
+
+        late_copy(i).start()
+
+    def late_take(name):
+        i = late_names.index(name)
+        late_copy(i).wait_recv()
+        left = F1[:, lefts[name] : lefts[name] + width]
+        mine[index[name]] = owners(dot_tn(left, r["own_late"].at[i].reshape(2 * rows, half)[...]))
+
+    dcq = narrow(r["dq_t"][...].T)
+    late_give("cqo", dcq)
+
+
+    def swap_copy(i):
+        return remote(
+            r["swap_send"].at[i], r["swap_recv"].at[i], r["pair_send"].at[8 + i], r["pair_recv"].at[8 + i], partner
+        )
+
+    for i, (name, ref) in enumerate((("cko", r["kb"]), ("cvo", r["vb"]))):
+        for c in range(2):
+            part = owners(dot_tn(r["encb"][...], ref[:, c * half : (c + 1) * half]))
+
+            @pl.when(core == c)
+            def _(part=part):
+                mine[index[name]] = part
+
+            @pl.when(core != c)
+            def _(part=part):
+                r["swap_send"][i] = part
+
+        swap_copy(i).start()
+
+    back, dg2 = rms_back(r["after_self"][...], gains["g2"], dot_nt(dcq, W["wcq"][...]))
+    grad = r["grad_cross"][...] + back
+    sb = narrow(grad)
+    late_give("so", sb)
+    late_take("cqo")
+    for i, name in enumerate(("cko", "cvo")):
+        swap_copy(i).wait_recv()
+
+        def one(o, carry, i=i, name=name):
+            to = mine.at[index[name]]
+            to[o] = narrow(to[o].astype(F32) + r["swap_recv"][i, o].astype(F32))
+            return carry
+
+        lax.fori_loop(0, n, one, 0)
+
+    gself = narrow(dot_nt(sb, W["wo"][...]))
+    dq_parts, dk_parts, dv_parts, sums = [], [], [], []
+    for pair in range(pairs):
+        at, masked, chances = self_chances(pair)
+        gmasked = pair_mask(gself[:, at])
+        dv_parts.append(narrow(dot_nn(narrow(chances), gmasked)))
+        dp = dot_nt(r["v"][:, at], gmasked)
+        ds = chances * (dp - jnp.sum(chances * dp, axis=0, keepdims=True))
+        sums.append(diagonal_sums(ds[:, :rows]))
+        sums.append(diagonal_sums(ds[:, rows:]))
+        dsb = narrow(ds)
+        dk_parts.append(narrow(dot_nn(dsb, masked)))
+        dq_parts.append(pair_diag(dot_tn(r["k"][:, at], dsb), rows))
+    dq = narrow(jnp.concatenate(dq_parts, axis=0).T)
+    dk = jnp.concatenate(dk_parts, axis=1)
+    dv = jnp.concatenate(dv_parts, axis=1)
+    late_give("sq", dq)
+    late_give("sk", dk)
+    late_give("sv", dv)
+    late_take("so")
+    into = dot_nt(dq, W["wq"][...]) + dot_nt(dk, W["wk"][...]) + dot_nt(dv, W["wv"][...])
+    late_take("sq")
+    late_take("sk")
+    late_take("sv")
+    back, dg1 = rms_back(hidden[...].astype(F32), gains["g1"], into)
+    r["hidden_out"][...] = grad + back
+    onehot = bucket_onehot_rows(table.shape[1], rows)
+    dtable = lax.dot_general(
+        jnp.concatenate(sums, axis=0), onehot, (((1,), (1,)), ((), ())), precision=lax.Precision.HIGHEST,
+        preferred_element_type=F32,
+    )
+
+    small_g, small_t = r["small_g"], r["small_t"]
+
+    def small_copies(step):
+        device = partner if step == bits else (me ^ (1 << step), core)
+        return [
+            remote(ref.at[step], ref.at[bits + 1 + step], r["small_send"].at[j, step], r["small_recv"].at[j, step], device)
+            for j, ref in enumerate((small_g, small_t))
+        ]
+
+    small_g[0] = jnp.concatenate([dg1, dg2, dg3, jnp.zeros((5, width), F32)], axis=0)
+    small_t[0] = jnp.zeros(small_t.shape[1:], F32)
+    small_t[0, : table.shape[0], : table.shape[1]] = dtable
+    for copy in small_copies(0):
+        copy.start()
+
+    def small_step(step):
+        for copy in small_copies(step):
+            copy.wait_recv()
+        for ref in (small_g, small_t):
+            total = ref[step] + ref[bits + 1 + step]
+            if step < bits:
+                ref[step + 1] = total
+            elif ref is small_t:
+                r["table_out"][...] = total[: table.shape[0], : table.shape[1]]
+            else:
+                for j, name in enumerate(("gs", "gc", "gf")):
+                    own = jnp.zeros((1, share), F32)
+                    for o in range(n):
+                        own = jnp.where(me == o, total[j : j + 1, o * share : (o + 1) * share], own)
+                    r[name][...] = own
+        if step < bits:
+            for copy in small_copies(step + 1):
+                copy.start()
+
+    early = count_in + count_out + 1
+    step = 0
+    for kind, piece, stage in drain_order(bits, early, pieces):
+        if kind == "begin":
+            begin(piece)
+        elif kind == "arrive":
+            arrive(piece, stage)
+        elif step <= bits:
+            small_step(step)
+            step += 1
+    for left in range(step, bits + 1):
+        small_step(left)
+    for piece in range(pieces):
+        last_copy(piece).wait_recv()
+        total = r["last_other"][piece].astype(F32)
+        for c in range(2):
+
+            @pl.when(core != c)
+            def _(c=c, total=total, piece=piece):
+                put(piece, c, total)
+
+    def others(d, carry):
+        q = me ^ d
+        remote(r["eg"].at[pl.ds(0, slot)], r["enc_out"].at[q], r["a2a_send"].at[q], r["a2a_recv"].at[q], (q, core)).wait_recv()
+        return carry
+
+    lax.fori_loop(1, n, others, 0)
+
+    def sent(p, carry):
+        send_back(p, True)
+        return carry
+
+    lax.fori_loop(0, n, sent, 0)
+
+    def brought(d, carry):
+        bring(me ^ d).wait_send()
+        return carry
+
+    lax.fori_loop(1, n, brought, 0)
+    for i in range(3):
+        pair_copy(i).wait_send()
+    for i in range(5):
+        late_copy(i).wait_send()
+    for i in range(2):
+        swap_copy(i).wait_send()
+    for piece in range(pieces):
+        for stage in range(bits):
+            stage_copy(piece, stage).wait_send()
+        last_copy(piece).wait_send()
+    for step in range(bits + 1):
+        for copy in small_copies(step):
+            copy.wait_send()
+
+
+def layer(n, slot, args):
+    rows, width = args["hidden"].shape
+    units = args["w_in"].shape[1]
+    share, half = width // n, width // 2
+    bits = n.bit_length() - 1
+    pairs = width // (2 * HD)
+    keys = n * slot
+    count_in = count_out = units // width
+    pieces = 8 + count_in + count_out
+    table = args["table"].shape
+    in_hbm = ("encodings", "w_in", "w_out") + SQUARES
+    vmem = pl.BlockSpec(memory_space=pltpu.VMEM)
+    anyw = pl.BlockSpec(memory_space=pl.ANY)
+    in_specs = [pl.BlockSpec(memory_space=pltpu.SMEM)] + [anyw if name in in_hbm else vmem for name in INPUTS[1:]]
+    wide = jax.ShapeDtypeStruct((rows, width), F32)
+    square = jax.ShapeDtypeStruct((share, width), F32)
+    gain = jax.ShapeDtypeStruct((1, share), F32)
+    outs = [wide, wide, jax.ShapeDtypeStruct((n, slot, width), BF)] + [square] * 8
+    outs += [jax.ShapeDtypeStruct((share, units), F32), jax.ShapeDtypeStruct((count_out * share, width), F32)]
+    outs += [gain] * 3 + [jax.ShapeDtypeStruct(table, F32)]
+    out_specs = [vmem, vmem, anyw] + [vmem] * 14
+    dma = pltpu.SemaphoreType.DMA
+    sixteen, full = pltpu.VMEM((rows, width), BF), pltpu.VMEM((rows, width), F32)
+    stat, masks = pltpu.VMEM((pairs, 2 * rows), F32), pltpu.VMEM((pairs, 2 * rows, 2 * HD), BF)
+    scratch = [
+        pltpu.VMEM((2, rows, 3 * width), BF),
+        pltpu.VMEM((2, rows, units + 2 * width), BF),
+        pltpu.VMEM((2, rows, units // 2 + width), BF),
+        pltpu.VMEM((rows, units // 2 + width), BF),
+        pltpu.VMEM((5, 2, rows, half), BF),
+        pltpu.VMEM((5, rows, half), BF),
+    ]
+    scratch += [pltpu.VMEM((keys, width), BF)] * 4
+    scratch += [pltpu.VMEM((8, width, width), BF), masks, masks, pltpu.VMEM((width, rows), F32)]
+    scratch += [sixteen] * 3 + [full] * 2 + [stat] * 3
+    scratch += [
+        pltpu.VMEM((2, n, share, half), BF),
+        pltpu.VMEM((2, n, share, half), BF),
+        pltpu.VMEM((pieces, n, share, half), BF),
+    ]
+    scratch += [pltpu.VMEM((pieces, n >> (b + 1), share, half), BF) for b in range(bits)]
+    scratch += [
+        pltpu.VMEM((pieces, share, half), BF),
+        pltpu.VMEM((pieces, share, half), BF),
+        pltpu.VMEM((2 * (bits + 1), 8, width), F32),
+        pltpu.VMEM((2 * (bits + 1), -(-table[0] // 8) * 8, 128), F32),
+        dma((8 + 3 * (units // half),)),
+        dma((10,)),
+        dma((10,)),
+        dma((pieces, bits)),
+        dma((pieces, bits)),
+        dma((n,)),
+        dma((n,)),
+        dma((n,)),
+        dma((n,)),
+        dma((1,)),
+        dma((2, bits + 1)),
+        dma((2, bits + 1)),
+        dma((pieces,)),
+        dma((pieces,)),
+    ]
+    return pl.pallas_call(
+        functools.partial(layer_kernel, n, slot, count_in, count_out),
+        out_shape=tuple(outs),
+        in_specs=in_specs,
+        out_specs=tuple(out_specs),
+        scratch_shapes=scratch,
+        compiler_params=pltpu.CompilerParams(collective_id=1, has_side_effects=True, vmem_limit_bytes=LAYER_LIMIT),
+    )(*[args[name] for name in INPUTS])
+
+
+def finish_kernel(count, *refs):
+    ins, outs, held, sems = refs[:count], refs[count : 2 * count], refs[2 * count : 3 * count], refs[-1]
+    into = [pltpu.make_async_copy(ins[i], held[i], sems.at[0, i]) for i in range(count)]
+    back = [pltpu.make_async_copy(held[i], outs[i], sems.at[1, i]) for i in range(count)]
+    for copy in into:
+        copy.start()
+    for i in range(count):
+        into[i].wait()
+        back[i].start()
+    for copy in back:
+        copy.wait()
+
+
+def finish(arrays):
+    count = len(arrays)
+    spec = pl.BlockSpec(memory_space=pl.ANY)
+    return pl.pallas_call(
+        functools.partial(finish_kernel, count),
+        out_shape=tuple(jax.ShapeDtypeStruct(a.shape, a.dtype) for a in arrays),
+        in_specs=[spec] * count,
+        out_specs=(spec,) * count,
+        scratch_shapes=[pltpu.VMEM(a.shape, a.dtype) for a in arrays] + [pltpu.SemaphoreType.DMA((2, count))],
+        compiler_params=pltpu.CompilerParams(vmem_limit_bytes=VMEM_LIMIT),
+    )(*arrays)
+
+
 def whole(shape=None):
     return pl.BlockSpec(memory_space=pltpu.VMEM)
 
@@ -530,6 +1220,19 @@
     cot = cotangent.reshape(rows, width)
     g1, g2, g3 = (gain.reshape(1, width) for gain in (gain_self, gain_cross, gain_feed))
     length_row = lengths.reshape(passages)
+    share = width // n
+    fits = passages == n and keys * width * 8 <= 16 << 20 and units == 4 * width
+    if n & (n - 1) == 0 and n >= 4 and share % 16 == 0 and fits:
+        out = layer(n, slot, dict(
+            lengths=length_row, encodings=encodings.reshape(n, slot, width), wq=wq, wk=wk, wv=wv, wo=wo, wcq=wcq, wck=wck,
+            wcv=wcv, wco=wco, w_in=w_in, w_out=w_out, hidden=own, cot=cot, g1=gain_self, g2=gain_cross,
+            g3=gain_feed, table=table.T,
+        ))
+        out = finish(out)
+        rows_out = tuple(o.reshape(hidden.shape) for o in out[:2])
+        gains = tuple(gain.reshape(share) for gain in out[13:16])
+        return rows_out + (out[2].reshape(encodings.shape),) + tuple(out[3:13]) + gains + (out[16].T,)
+
     source = lax.all_to_all(encodings, "pass", split_axis=2, concat_axis=0, tiled=True).reshape(keys, width)
 
     sixteen, wide = ((rows, width), BF), ((rows, width), F32)
@@ -607,7 +1310,6 @@
         own, h1, q, k, v, mix1, after_self, h2, dcq, grad_cross, wq, wk, wv, wo, wcq, g1, g2, table,
     )
 
-    share = width // n
     if n & (n - 1) == 0 and share % 16 == 0:
         squares = [d_q, d_k, d_v, d_so, d_cq, d_ck, d_cv, d_co]
         parts = [d.reshape(n, share, width) for d in squares]

time: 378 us -> 244 us (0.65)
  waiting for transfers between devices: 62.4 us -> 0 us
  Pallas kernels: 281 us -> 243 us
  local copies, waits for them, and re-layouts: 20.5 us -> 0 us
  starting transfers between devices: 11.7 us -> 0 us
    all_to_all x2 -> x0, waiting for transfers between devices: 62.4 us -> none  [the longest x1 62.4 us: per_device(): lax.all_to_all(encodings, 'pass', split_axis=2, concat_axis=0, tiled=True)]
    pallas_call x6 -> x2, Pallas kernels: 281 us -> 243 us  [the longest x1 238 us: layer(): pl.pallas_call(functools.partial(layer_kernel, n, slot, count_in, count_o...]
    all_to_all x2 -> x0, starting transfers between devices: 11.7 us -> none  [the longest x1 6.75 us: per_device(): lax.all_to_all(encodings, 'pass', split_axis=2, concat_axis=0, tiled=True)]
    slice x4 -> x0, local copies, waits for them, and re-layouts: 8.11 us -> none  [the longest x1 4.61 us: per_device(): parts += [d_in[i].reshape(n, share, width) for i in range(pieces)]]
    unnamed x15 -> x0, local copies, waits for them, and re-layouts: 4.72 us -> none
  transfers between devices with their start and end apart: 2 -> 0, of which waited for: 1 -> 0; matrix products, arithmetic and copies ran while one was open for 5% -> 0% of each run, Pallas kernels for 59% -> 0%
where the time goes in v2:
time: 244 us
  Pallas kernels  243 us (100%)
    pallas_call x1, Pallas kernels, layer(): pl.pallas_call(functools.partial(layer_kernel, n, slot, count_in, count_o...  238 us
    pallas_call x1, Pallas kernels, finish(): pl.pallas_call(functools.partial(finish_kernel, count), out_shape=tuple((...  5.18 us

profile of v2, /device:TPU:13, one launch (start us, length us, event | category | flops | bytes accessed | tf_op | source)
XLA Modules:
  0.0 243.8 jit_solution(15672604810945066820)
XLA Ops:
  0.7 237.7 %shard_map.305 = (f32[128,768]{1,0:T(8,128)}, f32[128,768]{1,0:T(8,128)}, bf16[16,128,768]{2,1,0:T(8,128)(2,1)}, f32[48,768]{1,0:T(8,128)}, f32[48,768]{1,0:T(8,...) custom-call(s32[16]{0:T(128)} %bitcast.16, ...), custom_call_target="tpu_custom_call" | custom-call | tf_op jit(solution)/shard_map/pallas_call | solution.py:1159
  238.4 5.2 %shard_map.306 = (f32[128,768]{1,0:T(8,128)}, f32[128,768]{1,0:T(8,128)}, bf16[16,128,768]{2,1,0:T(8,128)(2,1)}, f32[48,768]{1,0:T(8,128)}, f32[48,768]{1,0:T(8,...) custom-call(f32[128,768]{1,0:T(8,128)} %get-tuple-element.51.refs_0_, ...), custom_call_target="tpu_custom_call" | custom-call | tf_op jit(solution)/shard_map/pallas_call | solution.py:1185

commit v3 on v1

--- a/solution.py
+++ b/solution.py
@@ -1,8 +1,8 @@
 import functools
+from typing import Any, NamedTuple
 
 import jax
 import jax.numpy as jnp
-import numpy as np
 from jax import lax
 from jax.experimental import pallas as pl
 from jax.experimental.pallas import tpu as pltpu
@@ -15,8 +15,11 @@
 BF = jnp.bfloat16
 F32 = jnp.float32
 MESH = pl.DeviceIdType.MESH
+PASS, CORE = "pass", "pb"
+PLANES_FIRST = (2, 3, 6, 7, 11)
 ROOT = 0.7978845608028654
 VMEM_LIMIT = 56 << 20
+LAYER_LIMIT = 64 << 20
 
 
 def narrow(value):
@@ -72,9 +75,9 @@
 
 
 def head_bias(table, rows):
-    onehot = bucket_onehot_rows(table.shape[0], rows)
+    onehot = bucket_onehot_rows(table.shape[1], rows)
     return lax.dot_general(
-        table, onehot, (((0,), (0,)), ((), ())), precision=lax.Precision.HIGHEST,
+        table, onehot, (((1,), (0,)), ((), ())), precision=lax.Precision.HIGHEST,
         preferred_element_type=F32,
     )
 
@@ -117,7 +120,7 @@
     q_out[...] = q
     k_out[...] = k
     v_out[...] = v
-    bias = head_bias(table[...], rows)
+    bias = head_bias(table[...].T, rows)
     allowed = causal_mask(rows)
     mixed = []
     for pair in range(pairs):
@@ -278,7 +281,7 @@
     sb = narrow(grad)
     d_o[...] = narrow(dot_tn(mix[...], sb))
     gmix = narrow(dot_nt(sb, wo[...]))
-    bias = head_bias(table[...], rows)
+    bias = head_bias(table[...].T, rows)
     allowed = causal_mask(rows)
     dq_parts, dk_parts, dv_parts, sums = [], [], [], []
     for pair in range(pairs):
@@ -319,187 +322,869 @@
     )
 
 
-def add_rows(left, right, dest):
-    count = dest.shape[0]
-
-    def one(index, carry):
-        dest[index] = narrow(left[index].astype(F32) + right[index].astype(F32))
-        return carry
-
-    lax.fori_loop(0, count, one, 0)
-
-
-def reduce_kernel(n, singles, grouped, *refs):
-    pieces = singles + grouped
-    ins = list(refs[:singles]) + [refs[singles].at[:, i] for i in range(grouped)]
-    small_in, out, small_out = refs[singles + 1 : singles + 4]
+def halving_order(bits, piece):
+    first = list(range(bits))
+    if sum(other in PLANES_FIRST for other in range(piece + 1)) % 2 != piece % 2:
+        first[0], first[1] = first[1], first[0]
+    return first[2:] + first[:2] if piece in PLANES_FIRST else first
+
+
+class Inputs(NamedTuple):
+    lengths: Any
+    encodings: Any
+    wq: Any
+    wk: Any
+    wv: Any
+    wo: Any
+    wcq: Any
+    wck: Any
+    wcv: Any
+    wco: Any
+    w_in: Any
+    w_out: Any
+    hidden: Any
+    cot: Any
+    g1: Any
+    g2: Any
+    g3: Any
+    table: Any
+
+
+class Outputs(NamedTuple):
+    result: Any
+    hidden: Any
+    enc: Any
+    sq: Any
+    sk: Any
+    sv: Any
+    so: Any
+    cq: Any
+    ck: Any
+    cv: Any
+    co: Any
+    fin: Any
+    fout: Any
+    gs: Any
+    gc: Any
+    gf: Any
+    table: Any
+
+
+class Scratch(NamedTuple):
+    left_self: Any
+    left_feed: Any
+    right: Any
+    give: Any
+    late: Any
+    late_give: Any
+    enc: Any
+    keys: Any
+    values: Any
+    queries: Any
+    grads: Any
+    stats: Any
+    weights: Any
+    masked: Any
+    gmasked: Any
+    acc: Any
+    q: Any
+    k: Any
+    v: Any
+    after_self: Any
+    grad_cross: Any
+    top: Any
+    lse: Any
+    delta: Any
+    swap_give: Any
+    swap_take: Any
+    mine: Any
+    last_own: Any
+    last_other: Any
+    small_gains: Any
+    small_table: Any
+    load: Any
+    pair_send: Any
+    pair_recv: Any
+    sum_send: Any
+    sum_recv: Any
+    in_send: Any
+    in_recv: Any
+    all_send: Any
+    all_recv: Any
+    own: Any
+    out: Any
+    small_send: Any
+    small_recv: Any
+    last_send: Any
+    last_recv: Any
+
+
+CO, CQ, SO, SQ, SK, SV, CK, CV = range(8)
+
+
+def layer_kernel(n, slot, count_in, count_out, *refs):
     bits = n.bit_length() - 1
-    scratch = refs[singles + 4 :]
-    mine, other, stages = scratch[0], scratch[1], scratch[2 : 2 + bits]
-    local_sem, send_sem, recv_sem, small_buf, small_send, small_recv, last_sem = scratch[2 + bits : 9 + bits]
-    half = pieces // 2
-    me, core = lax.axis_index("pass"), lax.axis_index("pb")
+    ins = Inputs(*refs[: len(Inputs._fields)])
+    outs = Outputs(*refs[len(ins) : len(ins) + len(Outputs._fields)])
+    scratch = refs[len(ins) + len(outs) :]
+    r, stages = Scratch(*scratch[: len(Scratch._fields)]), scratch[len(Scratch._fields) :]
+    mine, weights = r.mine, r.weights
+    share, half = mine.shape[2], mine.shape[3] // 2
+    pieces = 2 * mine.shape[0]
+    rows, width = ins.hidden.shape
+    units = count_out * width
+    span = count_in * half
+    pairs = width // (2 * HD)
+    two = 2 * HD
+    line = n // 4
+    me, core = lax.axis_index(PASS), lax.axis_index(CORE)
+    low = me % 4
     partner = (me, 1 - core)
-
-    barrier = pltpu.get_barrier_semaphore()
-    pl.semaphore_signal(barrier, inc=1, device_id=partner, device_id_type=MESH)
-    for bit in range(bits):
-        pl.semaphore_signal(barrier, inc=1, device_id=(me ^ (1 << bit), core), device_id_type=MESH)
-    pl.semaphore_wait(barrier, bits + 1)
+    wq, wk, wv, wo, wcq, wck, wcv, wco = (weights.at[i] for i in range(8))
+    g1, g2, g3 = (g[...].reshape(1, width) for g in (ins.g1, ins.g2, ins.g3))
 
     def remote(src, dst, send, recv, device):
         return pltpu.make_async_remote_copy(
             src_ref=src, dst_ref=dst, send_sem=send, recv_sem=recv, device_id=device, device_id_type=MESH
         )
 
-    def order(piece):
-        first = list(range(bits))
-        if piece % 2 and bits > 1:
-            first[0], first[1] = first[1], first[0]
-        return first
-
-    def split(ref, piece, stage):
-        done = order(piece)[:stage]
-        bit = order(piece)[stage]
-        low = 1 << len([b for b in range(bit) if b not in done])
-        count = n >> stage
-        view = ref.reshape(count // (2 * low), 2, low, ref.shape[-2], ref.shape[-1])
-        return view, (me >> bit) & 1, low, count // (2 * low), bit
-
-    def swap(i, c):
-        return remote(ins[2 * i + 1 - c], other.at[i], send_sem.at[i, 0], recv_sem.at[i, 0], partner)
-
-    def fetch(i, c):
-        return pltpu.make_async_copy(ins[2 * i + c], mine.at[i], local_sem.at[i])
-
-    for i in range(half):
+    def by_core(body):
         for c in range(2):
-
-            @pl.when(core == c)
-            def _(i=i, c=c):
-                swap(i, c).start()
-                fetch(i, c).start()
-
-    def source(i, stage):
-        return other.at[i] if stage == 0 else stages[stage - 1].at[i]
-
-    def stage_copy(i, stage):
-        view, value, low, high, bit = split(source(i, stage), i, stage)
-        dst = stages[stage].at[i].reshape(high, low, *mine.shape[-2:])
-        return remote(
-            view.at[:, 1 - value], dst, send_sem.at[i, stage + 1], recv_sem.at[i, stage + 1], (me ^ (1 << bit), core)
+            pl.when(core == c)(functools.partial(body, c))
+
+    def columns(pair):
+        return slice(pair * two, (pair + 1) * two)
+
+    parts = units // width
+    loads = [(w, weights.at[i]) for i, w in enumerate(ins[2:10])]
+    tiles = mine.reshape(2 * parts, width, width)
+    for j in range(parts):
+        at = slice(j * width, (j + 1) * width)
+        loads += [(ins.w_in.at[:, at], tiles.at[j]), (ins.w_out.at[at], tiles.at[parts + j])]
+
+    def load(i):
+        return pltpu.make_async_copy(loads[i][0], loads[i][1], r.load.at[i])
+
+    for i in range(8):
+        load(i).start()
+
+    barrier = pltpu.get_barrier_semaphore()
+    pl.semaphore_signal(barrier, inc=1, device_id=partner, device_id_type=MESH)
+
+    def greet(d, carry):
+        pl.semaphore_signal(barrier, inc=1, device_id=(me ^ d, core), device_id_type=MESH)
+        return carry
+
+    lax.fori_loop(1, n, greet, 0)
+    pl.semaphore_wait(barrier, n)
+
+    def passage_at(p):
+        return pl.ds(pl.multiple_of(p * slot, slot), slot)
+
+    def bring(q):
+        return remote(ins.encodings.at[q], r.enc.at[passage_at(me)], r.in_send.at[q], r.in_recv.at[me], (q, core))
+
+    def arrived(p):
+        return remote(ins.encodings.at[p], r.enc.at[passage_at(p)], r.in_send.at[p], r.in_recv.at[p], (p, core))
+
+    def bring_range(first, last):
+        def one(d, carry):
+            bring(me ^ d).start()
+            return carry
+
+        lax.fori_loop(first, last, one, 0)
+
+    bring_range(1, 4)
+    own_passage = pltpu.make_async_copy(ins.encodings.at[me], r.enc.at[passage_at(me)], r.own.at[0])
+    own_passage.start()
+    for i in range(8, len(loads)):
+        load(i).start()
+
+    x_peer, y_peer = (me ^ 1, core), (me ^ 2, core)
+
+    steps_of_line = [[k for k in range(1, line) if k.bit_count() == hops] for hops in range(1, bits - 1)]
+    line_bits = len(steps_of_line)
+
+    def line_copy(kind, k):
+        last = k & -k
+        origin = me ^ (4 * (k ^ last))
+        ref = r.stats.at[origin] if kind == 2 else (r.queries, r.grads)[kind].at[:, origin]
+        return remote(ref, ref, r.all_send.at[kind, k - 1], r.all_recv.at[kind, k - 1], (me ^ (4 * last), core))
+
+    def spread_line(kind, number):
+        if number:
+            for k in steps_of_line[number - 1]:
+                line_copy(kind, k).wait_recv()
+        for k in reversed(steps_of_line[number]) if number < line_bits else ():
+            line_copy(kind, k).start()
+
+    def plane_copy(kind, number, k):
+        part = number % 2
+        first, second = (x_peer, y_peer) if part == 0 else (y_peer, x_peer)
+        origin = me ^ (4 * k) if number < 4 else me ^ (4 * k) ^ (1 << part)
+        at = (r.queries, r.grads)[kind].at[part, origin]
+        sem = line - 1 + number * line + k
+        return remote(at, at, r.all_send.at[kind, sem], r.all_recv.at[kind, sem], first if number < 2 else second)
+
+    def stat_plane(d):
+        view = r.stats.reshape(line, 4, *r.stats.shape[1:]).at[:, low]
+        sem = line - 2 + d
+        return remote(view, view, r.all_send.at[2, sem], r.all_recv.at[2, sem], (me ^ d, core))
+
+    def spread_plane(kind, blocks):
+        for number in range(4):
+            for k in blocks:
+                plane_copy(kind, number, k).start()
+
+    def spread_rest(kind, blocks):
+        for k in blocks:
+            for number in range(2):
+                plane_copy(kind, number, k).wait_recv()
+        for k in blocks:
+            for number in range(4, 6):
+                plane_copy(kind, number, k).start()
+
+    def spread_taken(kind):
+        for number in range(2, 6):
+            for k in range(line):
+                plane_copy(kind, number, k).wait_recv()
+
+    def spread_sent(kind):
+        for k in range(1, line):
+            line_copy(kind, k).wait_send()
+        for number in range(6):
+            for k in range(line):
+                plane_copy(kind, number, k).wait_send()
+
+    value = ins.hidden[...].astype(F32)
+    h1 = narrow(rms(value, g1))
+    r.left_self[0, :, :width] = h1
+    for i, ref in enumerate((r.q, r.k, r.v)):
+        load(i).wait()
+        ref[...] = narrow(dot_nn(h1, weights[i]))
+    bias = head_bias(ins.table[...], rows)
+    allowed = causal_mask(rows)
+
+    def self_chances(pair):
+        at = columns(pair)
+        masked = pair_mask(r.q[:, at])
+        scores = dot_nt(r.k[:, at], masked)
+        both = jnp.concatenate([toeplitz(bias[2 * pair + i : 2 * pair + i + 1], rows) for i in range(2)], axis=1)
+        scores = jnp.where(allowed, scores + both, NEG)
+        raised = jnp.exp(scores - jnp.max(scores, axis=0, keepdims=True))
+        return at, masked, raised / jnp.sum(raised, axis=0, keepdims=True)
+
+    for pair in range(pairs):
+        at, _, chances = self_chances(pair)
+        r.acc[at, :] = pair_diag(dot_tn(r.v[:, at], narrow(chances)), rows)
+    mix1 = narrow(r.acc[...].T)
+    r.left_self[0, :, 2 * width :] = mix1
+    load(3).wait()
+    after_self = value + dot_nn(mix1, wo[...])
+    r.after_self[...] = after_self
+    h2 = narrow(rms(after_self, g2))
+    r.left_self[0, :, width : 2 * width] = h2
+    load(4).wait()
+    cq = narrow(dot_nn(h2, wcq[...]))
+    for c in range(2):
+        r.queries[c, me] = cq[:, c * half : (c + 1) * half]
+    spread_line(0, 0)
+    bring_range(n // 2, 3 * n // 4)
+    for pair in range(pairs):
+        r.masked[pair] = pair_mask(cq[:, columns(pair)])
+    r.top[...] = jnp.full(r.top.shape, NEG, F32)
+    r.lse[...] = jnp.zeros(r.lse.shape, F32)
+    r.acc[...] = jnp.zeros(r.acc.shape, F32)
+
+    def pair_copy(i):
+        src = (r.left_self.at[0], r.left_feed.at[0], r.give)[i]
+        dst = (r.left_self, r.left_feed, r.right)[i].at[1]
+        return remote(src, dst, r.pair_send.at[i], r.pair_recv.at[i], partner)
+
+    pair_copy(0).start()
+
+    place = lax.broadcasted_iota(jnp.int32, (slot, 2 * rows), 0)
+
+    def spread(row):
+        return jnp.concatenate(
+            [jnp.broadcast_to(row[:, :rows], (HD, rows)), jnp.broadcast_to(row[:, rows:], (HD, rows))], axis=0
         )
 
-    def small_copy(stage):
-        device = partner if stage == bits else (me ^ (1 << stage), core)
-        return remote(small_buf.at[stage], small_buf.at[bits + 1 + stage], small_send.at[stage], small_recv.at[stage], device)
-
-    small_buf[0] = small_in[...]
-    small_copy(0).start()
-
-    def last_copy(i):
-        return remote(out_buf(i), out_buf2(i), last_sem.at[0, i], last_sem.at[1, i], partner)
-
-    out_own, out_other = scratch[-2], scratch[-1]
-
-    def out_buf(i):
-        return out_own.at[i]
-
-    def out_buf2(i):
-        return out_other.at[i]
-
-    for tick in range(half + bits + 1):
-        for stage in reversed(range(bits + 1)):
-            i = tick - stage
-            if not 0 <= i < half:
-                continue
-            if stage == 0:
-                for c in range(2):
-
-                    @pl.when(core == c)
-                    def _(i=i, c=c):
-                        fetch(i, c).wait()
-
-                swap(i, 0).wait_recv()
-                add_rows(mine.at[i], other.at[i], other.at[i])
+    load(5).wait()
+    load(6).wait()
+    own_passage.wait()
+    few = 2
+    turns = n // few
+
+    def forward_block(turn, carry):
+        @pl.when(turn == 1)
+        def _():
+            for number in range(1, line_bits):
+                spread_line(0, number)
+            bring_range(3 * n // 4, n)
+            bring_range(4, n // 2)
+
+        @pl.when(turn == 3)
+        def _():
+            spread_line(0, line_bits)
+            spread_plane(0, range(line))
+
+        pl.when(turn == turns - 2)(functools.partial(spread_rest, 0, range(line)))
+        part = turn // (turns // 4)
+        moved = turn % (turns // 4) + (part % 2 * 2 + part // 2) * (turns // 4)
+        first = (moved ^ (me // few)) * few
+        for i in range(few):
+
+            @pl.when(first + i != me)
+            def _(i=i):
+                arrived(first + i).wait_recv()
+
+        at = pl.ds(pl.multiple_of(first * slot, few * slot), few * slot)
+        source = r.enc[at]
+        r.keys[at] = narrow(dot_nn(source, wck[...]))
+        r.values[at] = narrow(dot_nn(source, wcv[...]))
+        valid = jnp.concatenate([place < ins.lengths[first + i] for i in range(few)], axis=0)
+        for pair in range(pairs):
+            cols = columns(pair)
+            scores = jnp.where(valid, dot_nt(r.keys[at, cols], r.masked[pair]), NEG)
+            before = r.top[pair : pair + 1]
+            now = jnp.maximum(before, jnp.max(scores, axis=0, keepdims=True))
+            r.top[pair : pair + 1] = now
+            fade = jnp.exp(before - now)
+            raised = jnp.exp(scores - now)
+            r.lse[pair : pair + 1] = r.lse[pair : pair + 1] * fade + jnp.sum(raised, axis=0, keepdims=True)
+            part = pair_diag(dot_tn(r.values[at, cols], narrow(raised)), rows)
+            r.acc[cols, :] = r.acc[cols, :] * spread(fade) + part
+        return carry
+
+    lax.fori_loop(0, turns, forward_block, 0)
+    for pair in range(pairs):
+        cols = columns(pair)
+        sums = r.lse[pair : pair + 1]
+        r.lse[pair : pair + 1] = r.top[pair : pair + 1] + jnp.log(sums)
+        r.acc[cols, :] = r.acc[cols, :] * spread(1.0 / sums)
+
+    own_load = pltpu.make_async_copy(ins.encodings, r.enc.reshape(n, slot, width), r.own.at[0])
+    own_load.start()
+    mix2 = narrow(r.acc[...].T)
+    r.left_feed[0, :, units + width :] = mix2
+    load(7).wait()
+    after_cross = r.after_self[...] + dot_nn(mix2, wco[...])
+    h3 = narrow(rms(after_cross, g3))
+    r.left_feed[0, :, units : units + width] = h3
+    cb = ins.cot[...]
+    result = after_cross
+    into = jnp.zeros((rows, width), F32)
+    for j in range(parts):
+        load(8 + 2 * j).wait()
+        inner = dot_nn(h3, tiles[j])
+        bent = jnp.tanh(ROOT * (inner + 0.044715 * (inner * inner * inner)))
+        active = narrow(0.5 * inner * (1.0 + bent))
+        r.left_feed[0, :, j * width : (j + 1) * width] = active
+        slope = 0.5 * (1.0 + bent) + (0.5 * ROOT) * inner * (1.0 - bent * bent) * (1.0 + (3 * 0.044715) * inner * inner)
+        load(9 + 2 * j).wait()
+        result = result + dot_nn(active, tiles[parts + j])
+        gi = narrow(dot_nt(cb, tiles[parts + j]) * slope)
+        to = slice((j % (parts // 2)) * width, (j % (parts // 2) + 1) * width)
+
+        def keep(c, gi=gi, to=to, owner=j // (parts // 2)):
+            if c == owner:
+                r.right[0, :, to] = gi
             else:
-                copy = stage_copy(i, stage - 1)
-                copy.wait_recv()
-                view, value, low, high, bit = split(source(i, stage - 1), i, stage - 1)
-                dst = stages[stage - 1].at[i]
-                if stage < bits:
-                    kept = view.at[:, value]
-
-                    def one(index, carry, kept=kept, dst=dst, low=low):
-                        dst[index] = narrow(kept[index // low, index % low].astype(F32) + dst[index].astype(F32))
-                        return carry
-
-                    lax.fori_loop(0, high * low, one, 0)
-                else:
-                    total = view[0, value, 0].astype(F32) + dst[0].astype(F32)
-                    out_own[i] = narrow(total)
-                    for c in range(2):
-
-                        @pl.when(core == c)
-                        def _(i=i, c=c, total=total):
-                            out[2 * i + c] = total
-
-            if stage < bits:
-                stage_copy(i, stage).start()
-            else:
-                last_copy(i).start()
-        if 1 <= tick <= bits + 1:
-            stage = tick - 1
-            small_copy(stage).wait_recv()
-            total = small_buf[stage] + small_buf[bits + 1 + stage]
-            if stage < bits:
-                small_buf[stage + 1] = total
-                small_copy(stage + 1).start()
-            else:
-                small_out[...] = total
-    for i in range(half):
-        last_copy(i).wait_recv()
+                r.give[:, to] = gi
+
+        by_core(keep)
+        into = into + dot_nt(gi, tiles[j])
+    outs.result[...] = result
+    pair_copy(1).start()
+    back, dg3 = rms_back(after_cross, g3, into)
+    grad = cb.astype(F32) + back
+    r.grad_cross[...] = grad
+    gb = narrow(grad)
+
+    def keep_columns(c):
+        for j, value in enumerate((cb, gb)):
+            to = slice(span + j * half, span + (j + 1) * half)
+            r.right[0, :, to] = value[:, c * half : (c + 1) * half]
+            r.give[:, to] = value[:, (1 - c) * half : (2 - c) * half]
+
+    by_core(keep_columns)
+    pair_copy(2).start()
+    gmix = narrow(dot_nt(gb, wco[...]))
+    for c in range(2):
+        r.grads[c, me] = gmix[:, c * half : (c + 1) * half]
+    spread_line(1, 0)
+    spread_plane(1, [0])
+    product = gmix.astype(F32).T * r.acc[...]
+    for pair in range(pairs):
+        at = columns(pair)
+        r.gmasked[pair] = pair_mask(gmix[:, at])
+        part = product[at]
+        r.delta[pair : pair + 1] = jnp.concatenate(
+            [jnp.sum(part[:HD], axis=0, keepdims=True), jnp.sum(part[HD:], axis=0, keepdims=True)], axis=1
+        )
+    lane = lax.broadcasted_iota(jnp.int32, (1, 2 * rows), 1)
+    extent = jnp.zeros((1, 2 * rows), F32)
+    for p in range(n):
+        extent = jnp.where(lane == p, ins.lengths[p].astype(F32), extent)
+    r.stats[me, :pairs] = r.lse[...]
+    r.stats[me, pairs : 2 * pairs] = r.delta[...]
+    r.stats[me, 2 * pairs : 2 * pairs + 1] = extent
+    spread_line(2, 0)
+    r.acc[...] = jnp.zeros(r.acc.shape, F32)
+
+    def lanes(piece):
+        return slice((piece % 2) * half, (piece % 2 + 1) * half)
+
+    def split(piece, stage):
+        done = halving_order(bits, piece)[:stage]
+        bit = halving_order(bits, piece)[stage]
+        inner = 1 << len([b for b in range(bit) if b not in done])
+        outer = (n >> stage) // (2 * inner)
+
+        def half_of(value):
+            if stage:
+                return stages[stage - 1].reshape(pieces, outer, 2, inner, share, half).at[piece, :, value]
+            return mine.reshape(pieces // 2, outer, 2, inner, share, 2 * half).at[piece // 2, :, value, :, :, lanes(piece)]
+
+        return half_of, (me >> bit) & 1, inner, outer, bit
+
+    def stage_copy(piece, stage):
+        half_of, value, inner, outer, bit = split(piece, stage)
+        dst = stages[stage].at[piece].reshape(outer, inner, share, half)
+        sems = r.sum_send.at[piece, stage], r.sum_recv.at[piece, stage]
+        return remote(half_of(1 - value), dst, *sems, (me ^ (1 << bit), core))
+
+    first_square = count_in + count_out
+    square_outs = (outs.co, outs.cq, outs.so, outs.sq, outs.sk, outs.sv, outs.ck, outs.cv)
+
+    def put(piece, c, total):
+        if piece < count_in:
+            outs.fin[:, (c * count_in + piece) * half : (c * count_in + piece + 1) * half] = total
+        elif piece < first_square:
+            k = piece - count_in
+            outs.fout[k * share : (k + 1) * share, c * half : (c + 1) * half] = total
+        else:
+            square_outs[piece - first_square][:, c * half : (c + 1) * half] = total
+
+    def last_copy(piece):
+        return remote(r.last_own.at[piece], r.last_other.at[piece], r.last_send.at[piece], r.last_recv.at[piece], partner)
+
+    def begin(piece):
+        stage_copy(piece, 0).start()
+
+    def arrive(piece, stage):
+        stage_copy(piece, stage).wait_recv()
+        half_of, value, inner, outer, _ = split(piece, stage)
+        kept = half_of(value)
+        dst = stages[stage].at[piece]
+        if stage + 1 < bits:
+
+            def one(i, carry):
+                dst[i] = narrow(kept[i // inner, i % inner].astype(F32) + dst[i].astype(F32))
+                return carry
+
+            lax.fori_loop(0, outer * inner, one, 0)
+            stage_copy(piece, stage + 1).start()
+        else:
+            total = kept[0, 0].astype(F32) + dst[0].astype(F32)
+            r.last_own[piece] = narrow(total)
+            last_copy(piece).start()
+            by_core(lambda c: put(piece, c, total))
+
+    def owners(value):
+        return narrow(value).reshape(n, share, half)
+
+    def keep_piece(piece, value):
+        mine[piece // 2, :, :, lanes(piece)] = value
+
+    for i in range(3):
+        pair_copy(i).wait_recv()
+    left_self, left_feed, right = (x.reshape(2 * rows, x.shape[2]) for x in (r.left_self, r.left_feed, r.right))
+    early = [piece for piece in range(first_square) if piece not in PLANES_FIRST]
+    for piece in range(count_in):
+        keep_piece(piece, owners(dot_tn(left_feed[:, units : units + width], right[:, piece * half : (piece + 1) * half])))
+        if piece in early[:2]:
+            begin(piece)
+    per = width // (count_out * share)
+    for part in range(count_out):
+        value = narrow(dot_tn(left_feed[:, part * width : (part + 1) * width], right[:, span : span + half]))
+        value = value.reshape(per, count_out, share, half)
+        for k in range(count_out):
+            piece = count_in + k
+            mine[piece // 2, part * per : (part + 1) * per, :, lanes(piece)] = value[:, k]
+    keep_piece(first_square + CO, owners(dot_tn(left_feed[:, units + width :], right[:, span + half :])))
+    for piece in early[2:]:
+        begin(piece)
+
+    many = 4
+
+    def question_block(turn, carry):
+        at = pl.ds(pl.multiple_of(turn * many * slot, many * slot), many * slot)
+        valid = jnp.concatenate([place < ins.lengths[turn * many + i] for i in range(many)], axis=0)
+        for pair in range(pairs):
+            cols = columns(pair)
+            key = r.keys[at, cols]
+            scores = jnp.where(valid, dot_nt(key, r.masked[pair]), NEG)
+            chances = jnp.exp(scores - r.lse[pair : pair + 1])
+            ds = narrow(chances * (dot_nt(r.values[at, cols], r.gmasked[pair]) - r.delta[pair : pair + 1]))
+            r.acc[cols, :] = r.acc[cols, :] + pair_diag(dot_tn(key, ds), rows)
+        return carry
+
+    lax.fori_loop(0, n // (2 * many), question_block, 0)
+
+    for number in range(1, line_bits):
+        spread_line(1, number)
+        spread_line(2, number)
+        spread_plane(1, steps_of_line[number - 1])
+    for piece in PLANES_FIRST:
+        if piece < first_square:
+            begin(piece)
+    lax.fori_loop(n // (2 * many), n // many, question_block, 0)
+
+    late = (CQ, SO, SQ, SK, SV)
+    lefts = (width, 2 * width, 0, 0, 0)
+
+    def late_copy(i):
+        return remote(r.late_give.at[i], r.late.at[i, 1], r.pair_send.at[3 + i], r.pair_recv.at[3 + i], partner)
+
+    def late_give(name, value):
+        i = late.index(name)
+
+        def part(c):
+            r.late[i, 0] = value[:, c * half : (c + 1) * half]
+            r.late_give[i] = value[:, (1 - c) * half : (2 - c) * half]
+
+        by_core(part)
+        late_copy(i).start()
+
+    def late_take(name, now=True):
+        i = late.index(name)
+        late_copy(i).wait_recv()
+        left = left_self[:, lefts[i] : lefts[i] + width]
+        keep_piece(first_square + name, owners(dot_tn(left, r.late.at[i].reshape(2 * rows, half)[...])))
+        if now:
+            begin(first_square + name)
+
+    dcq = narrow(r.acc[...].T)
+    late_give(CQ, dcq)
+    back, dg2 = rms_back(r.after_self[...], g2, dot_nt(dcq, wcq[...]))
+    grad = r.grad_cross[...] + back
+    sb = narrow(grad)
+    late_give(SO, sb)
+
+    own_load.wait()
+
+    def project(turn, carry):
+        at = pl.ds(pl.multiple_of(turn * many * slot, many * slot), many * slot)
+        source = r.enc[at]
+        r.keys[at] = narrow(dot_nn(source, wck[...]))
+        r.values[at] = narrow(dot_nn(source, wcv[...]))
+        return carry
+
+    lax.fori_loop(0, n // (2 * many), project, 0)
+    spread_rest(1, [0])
+    spread_line(1, line_bits)
+    spread_plane(1, steps_of_line[-1])
+    spread_line(2, line_bits)
+    for d in range(1, 4):
+        stat_plane(d).start()
+    for ks in steps_of_line[:-1]:
+        spread_rest(1, ks)
+    lax.fori_loop(n // (2 * many), n // many, project, 0)
+    late_take(CQ, False)
+
+    gself = narrow(dot_nt(sb, wo[...]))
+    dq_parts, dk_parts, dv_parts, sums = [], [], [], []
+    for pair in range(pairs):
+        at, masked, chances = self_chances(pair)
+        gmasked = pair_mask(gself[:, at])
+        dv_parts.append(narrow(dot_nn(narrow(chances), gmasked)))
+        dp = dot_nt(r.v[:, at], gmasked)
+        ds = chances * (dp - jnp.sum(chances * dp, axis=0, keepdims=True))
+        sums.append(diagonal_sums(ds[:, :rows]))
+        sums.append(diagonal_sums(ds[:, rows:]))
+        dsb = narrow(ds)
+        dk_parts.append(narrow(dot_nn(dsb, masked)))
+        dq_parts.append(pair_diag(dot_tn(r.k[:, at], dsb), rows))
+    dq = narrow(jnp.concatenate(dq_parts, axis=0).T)
+    dk = jnp.concatenate(dk_parts, axis=1)
+    dv = jnp.concatenate(dv_parts, axis=1)
+    late_give(SQ, dq)
+    late_give(SK, dk)
+    late_give(SV, dv)
+    late_take(SO, False)
+    into = dot_nt(dq, wq[...]) + dot_nt(dk, wk[...]) + dot_nt(dv, wv[...])
+    late_take(SQ, False)
+    late_take(SK, False)
+    late_take(SV, False)
+    back, dg1 = rms_back(ins.hidden[...].astype(F32), g1, into)
+    outs.hidden[...] = grad + back
+    onehot = bucket_onehot_rows(ins.table.shape[1], rows)
+    dtable = lax.dot_general(
+        jnp.concatenate(sums, axis=0), onehot, (((1,), (1,)), ((), ())), precision=lax.Precision.HIGHEST,
+        preferred_element_type=F32,
+    )
+
+    small = (r.small_gains, r.small_table)
+
+    def small_copies(step):
+        device = partner if step == bits else (me ^ (1 << step), core)
+        return [
+            remote(ref.at[step], ref.at[bits + 1 + step], r.small_send.at[j, step], r.small_recv.at[j, step], device)
+            for j, ref in enumerate(small)
+        ]
+
+    r.small_gains[0] = jnp.concatenate([dg1, dg2, dg3, jnp.zeros((5, width), F32)], axis=0)
+    r.small_table[0] = jnp.zeros(r.small_table.shape[1:], F32)
+    r.small_table[0, : dtable.shape[0], : dtable.shape[1]] = dtable
+    for copy in small_copies(0):
+        copy.start()
+
+    def small_step(step):
+        for copy in small_copies(step):
+            copy.wait_recv()
+        gains, table = (ref[step] + ref[bits + 1 + step] for ref in small)
+        if step < bits:
+            r.small_gains[step + 1] = gains
+            r.small_table[step + 1] = table
+            for copy in small_copies(step + 1):
+                copy.start()
+        else:
+            outs.table[...] = table[: dtable.shape[0], : dtable.shape[1]]
+            for j, out in enumerate((outs.gs, outs.gc, outs.gf)):
+                own = jnp.zeros((1, share), F32)
+                for o in range(n):
+                    own = jnp.where(me == o, gains[j : j + 1, o * share : (o + 1) * share], own)
+                out[...] = own
+
+    place_f = place.astype(F32)
+
+    def owner_block(turn, carry):
+        q = (turn % line) * 4 + (low ^ (turn // line))
+        at = passage_at(q)
+        stats = r.stats[q]
+        extent = jnp.sum(jnp.where(lane == me, stats[2 * pairs : 2 * pairs + 1], 0.0), axis=1, keepdims=True)
+        valid = place_f < extent
+        for pair in range(pairs):
+            cols = columns(pair)
+            c, within = pair // (pairs // 2), columns(pair % (pairs // 2))
+            masked, gmasked = pair_mask(r.queries[c, q, :, within]), pair_mask(r.grads[c, q, :, within])
+            scores = jnp.where(valid, dot_nt(r.keys[at, cols], masked), NEG)
+            chances = jnp.exp(scores - stats[pair : pair + 1])
+            ds = narrow(chances * (dot_nt(r.values[at, cols], gmasked) - stats[pairs + pair : pairs + pair + 1]))
+            r.values[at, cols] = narrow(dot_nn(narrow(chances), gmasked))
+            r.keys[at, cols] = narrow(dot_nn(ds, masked))
+        return carry
+
+    spread_rest(1, steps_of_line[-1])
+
+    middle, last = range(first_square, first_square + CK), range(first_square + CK, pieces)
+
+    def taken_up(event):
+        piece, stage = event
+        if piece in early:
+            keys = (0.0, 1.1, 3.0, 4.3)
+        elif piece in last:
+            keys = (3.5, 3.8, 4.2, 4.9)
+        elif piece not in middle:
+            keys = (0.5 if piece < count_in else 1.0, 3.3, 3.9, 4.4)
+        elif piece in PLANES_FIRST:
+            keys = (3.25, 3.75, 4.1, 4.7)
+        elif piece == first_square + SV:
+            keys = (3.05, 3.85, 4.25, 4.75)
+        elif piece == first_square + SK:
+            keys = (2.1, 3.35, 3.65, 4.65)
+        else:
+            keys = (2.0, 3.1, 3.6, 4.6)
+        return keys[min(stage, 2)] if stage + 1 < bits else keys[3]
+
+    events = sorted(((piece, stage) for piece in range(pieces) for stage in range(bits)), key=taken_up)
+    visits = [[event for event in events if min(int(taken_up(event)), 3) == visit] for visit in range(4)]
+    for piece, stage in visits[0]:
+        arrive(piece, stage)
+    for piece in middle:
+        begin(piece)
+
+    lax.fori_loop(0, line, owner_block, 0)
+
+    spread_taken(0)
+    spread_taken(1)
+    for d in range(1, 4):
+        stat_plane(d).wait_recv()
+    lax.fori_loop(line, 2 * line, owner_block, 0)
+    small_step(0)
+    for piece, stage in visits[1]:
+        arrive(piece, stage)
+    lax.fori_loop(2 * line, n, owner_block, 0)
+    for piece, stage in visits[2]:
+        arrive(piece, stage)
+
+    def encoding_block(turn):
+        at = slice(turn * many * slot, (turn + 1) * many * slot)
+        value = narrow(dot_nt(r.keys[at], wck[...]) + dot_nt(r.values[at], wcv[...]))
         for c in range(2):
-
-            @pl.when(core == c)
-            def _(i=i, c=c):
-                out[2 * i + 1 - c] = out_other[i].astype(F32)
-
-    for i in range(half):
-        swap(i, 0).wait_send()
+            to = slice(turn * many, (turn + 1) * many)
+            r.grads[c, to] = value[:, c * half : (c + 1) * half].reshape(many, slot, half)
+
+    def out_copy(c):
+        return pltpu.make_async_copy(r.grads.at[c], outs.enc.at[:, :, c * half : (c + 1) * half], r.out.at[c])
+
+    spread_sent(0)
+    spread_sent(1)
+
+    def swap_copy(i):
+        return remote(r.swap_give.at[i], r.swap_take.at[i], r.pair_send.at[8 + i], r.pair_recv.at[8 + i], partner)
+
+    def columns_of(ref, c):
+        return owners(dot_tn(r.enc[...], ref[:, pl.ds(pl.multiple_of(c * half, 128), half)]))
+
+    for i, ref in enumerate((r.keys, r.values)):
+        r.swap_give[i] = columns_of(ref, 1 - core)
+        swap_copy(i).start()
+    for i, (name, ref) in enumerate(((CK, r.keys), (CV, r.values))):
+        piece = first_square + name
+        keep_piece(piece, columns_of(ref, core))
+        swap_copy(i).wait_recv()
+
+        def one(o, carry, i=i, to=mine.at[piece // 2, :, :, lanes(piece)]):
+            to[o] = narrow(to[o].astype(F32) + r.swap_take[i, o].astype(F32))
+            return carry
+
+        lax.fori_loop(0, n, one, 0)
+        begin(piece)
+
+    rest = visits[3]
+    for number, (piece, stage) in enumerate(rest):
+        if (piece, stage) == (last[0], 0):
+            for turn in range(n // many):
+                encoding_block(turn)
+            for c in range(2):
+                out_copy(c).start()
+        arrive(piece, stage)
+        for step in range(1, bits + 1):
+            if (piece, stage) == (last[1], step - 1):
+                small_step(step)
+
+    for piece in range(pieces):
+        last_copy(piece).wait_recv()
+        total = r.last_other[piece].astype(F32)
+        by_core(lambda c: put(piece, 1 - c, total))
+
+    for c in range(2):
+        out_copy(c).wait()
+
+    def brought(d, carry):
+        bring(me ^ d).wait_send()
+        return carry
+
+    lax.fori_loop(1, n, brought, 0)
+    for k in range(1, line):
+        line_copy(2, k).wait_send()
+    for d in range(1, 4):
+        stat_plane(d).wait_send()
+    for i in range(3):
+        pair_copy(i).wait_send()
+    for i in range(5):
+        late_copy(i).wait_send()
+    for i in range(2):
+        swap_copy(i).wait_send()
+    for piece in range(pieces):
         for stage in range(bits):
-            stage_copy(i, stage).wait_send()
-        last_copy(i).wait_send()
-    for stage in range(bits + 1):
-        small_copy(stage).wait_send()
-
-
-def reduce_all(n, parts, group, small):
-    pieces = len(parts) + group.shape[1]
-    half = pieces // 2
-    _, rows, width = parts[0].shape
+            stage_copy(piece, stage).wait_send()
+        last_copy(piece).wait_send()
+    for step in range(bits + 1):
+        for copy in small_copies(step):
+            copy.wait_send()
+
+
+def layer(n, slot, args):
+    rows, width = args.hidden.shape
+    units = args.w_in.shape[1]
+    share, half = width // n, width // 2
     bits = n.bit_length() - 1
-    stage_shapes = [pltpu.VMEM((half, n >> (s + 1), rows, width), BF) for s in range(bits)]
+    pairs = width // (2 * HD)
+    keys = n * slot
+    count_in = count_out = units // width
+    pieces = 8 + count_in + count_out
+    table = args.table.shape
+    vmem, hbm = pl.BlockSpec(memory_space=pltpu.VMEM), pl.BlockSpec(memory_space=pl.ANY)
+    in_specs = [pl.BlockSpec(memory_space=pltpu.SMEM)] + [hbm] * 11 + [vmem] * 6
+    wide = jax.ShapeDtypeStruct((rows, width), F32)
+    square = jax.ShapeDtypeStruct((share, width), F32)
+    gain = jax.ShapeDtypeStruct((1, share), F32)
+    results = [wide, wide, jax.ShapeDtypeStruct((n, slot, width), BF)] + [square] * 8
+    results += [jax.ShapeDtypeStruct((share, units), F32), jax.ShapeDtypeStruct((count_out * share, width), F32)]
+    results += [gain] * 3 + [jax.ShapeDtypeStruct(table, F32)]
+    dma = pltpu.SemaphoreType.DMA
+    sixteen, full = pltpu.VMEM((rows, width), BF), pltpu.VMEM((rows, width), F32)
+    stat, masks = pltpu.VMEM((pairs, 2 * rows), F32), pltpu.VMEM((pairs, 2 * rows, 2 * HD), BF)
+    blocks, shared = pltpu.VMEM((keys, width), BF), pltpu.VMEM((2, n, rows, half), BF)
+    swap = pltpu.VMEM((2, n, share, half), BF)
+    last = pltpu.VMEM((pieces, share, half), BF)
+    up = lambda count: -(-count // 8) * 8
+    scratch = Scratch(
+        left_self=pltpu.VMEM((2, rows, 3 * width), BF),
+        left_feed=pltpu.VMEM((2, rows, units + 2 * width), BF),
+        right=pltpu.VMEM((2, rows, units // 2 + width), BF),
+        give=pltpu.VMEM((rows, units // 2 + width), BF),
+        late=pltpu.VMEM((5, 2, rows, half), BF),
+        late_give=pltpu.VMEM((5, rows, half), BF),
+        enc=blocks, keys=blocks, values=blocks, queries=shared, grads=shared,
+        stats=pltpu.VMEM((n, up(2 * pairs + 1), 2 * rows), F32),
+        weights=pltpu.VMEM((8, width, width), BF),
+        masked=masks, gmasked=masks,
+        acc=pltpu.VMEM((width, rows), F32),
+        q=sixteen, k=sixteen, v=sixteen, after_self=full, grad_cross=full,
+        top=stat, lse=stat, delta=stat, swap_give=swap, swap_take=swap,
+        mine=pltpu.VMEM((pieces // 2, n, share, width), BF),
+        last_own=last, last_other=last,
+        small_gains=pltpu.VMEM((2 * (bits + 1), 8, width), F32),
+        small_table=pltpu.VMEM((2 * (bits + 1), up(table[0]), 128), F32),
+        load=dma((8 + 2 * (units // width),)),
+        pair_send=dma((10,)), pair_recv=dma((10,)),
+        sum_send=dma((pieces, bits)), sum_recv=dma((pieces, bits)),
+        in_send=dma((n,)), in_recv=dma((n,)),
+        all_send=dma((3, 7 * (n // 4))), all_recv=dma((3, 7 * (n // 4))),
+        own=dma((1,)), out=dma((2,)),
+        small_send=dma((2, bits + 1)), small_recv=dma((2, bits + 1)),
+        last_send=dma((pieces,)), last_recv=dma((pieces,)),
+    )
+    stages = [pltpu.VMEM((pieces, n >> (b + 1), share, half), BF) for b in range(bits)]
     return pl.pallas_call(
-        functools.partial(reduce_kernel, n, len(parts), group.shape[1]),
-        out_shape=(jax.ShapeDtypeStruct((pieces, rows, width), F32), jax.ShapeDtypeStruct(small.shape, F32)),
-        in_specs=[pl.BlockSpec(memory_space=pl.ANY)] * (len(parts) + 1) + [pl.BlockSpec(memory_space=pltpu.VMEM)],
-        out_specs=(pl.BlockSpec(memory_space=pltpu.VMEM), pl.BlockSpec(memory_space=pltpu.VMEM)),
-        scratch_shapes=[pltpu.VMEM((half, n, rows, width), BF), pltpu.VMEM((half, n, rows, width), BF)]
-        + stage_shapes
-        + [
-            pltpu.SemaphoreType.DMA((half,)),
-            pltpu.SemaphoreType.DMA((half, bits + 1)),
-            pltpu.SemaphoreType.DMA((half, bits + 1)),
-            pltpu.VMEM((2 * (bits + 1),) + small.shape, F32),
-            pltpu.SemaphoreType.DMA((bits + 1,)),
-            pltpu.SemaphoreType.DMA((bits + 1,)),
-            pltpu.SemaphoreType.DMA((2, half)),
-            pltpu.VMEM((half, rows, width), BF),
-            pltpu.VMEM((half, rows, width), BF),
-        ],
-        compiler_params=pltpu.CompilerParams(collective_id=0, has_side_effects=True, vmem_limit_bytes=VMEM_LIMIT),
-    )(*parts, group, small)
+        functools.partial(layer_kernel, n, slot, count_in, count_out),
+        out_shape=tuple(results),
+        in_specs=in_specs,
+        out_specs=tuple([vmem, vmem, hbm] + [vmem] * 14),
+        scratch_shapes=list(scratch) + stages,
+        compiler_params=pltpu.CompilerParams(collective_id=1, has_side_effects=True, vmem_limit_bytes=LAYER_LIMIT),
+    )(*args)
+
+
+def finish_kernel(count, *refs):
+    ins, outs, held, sems = refs[:count], refs[count : 2 * count], refs[2 * count : 3 * count], refs[-1]
+    into = [pltpu.make_async_copy(ins[i], held[i], sems.at[0, i]) for i in range(count)]
+    back = [pltpu.make_async_copy(held[i], outs[i], sems.at[1, i]) for i in range(count)]
+    for copy in into:
+        copy.start()
+    for i in range(count):
+        into[i].wait()
+        back[i].start()
+    for copy in back:
+        copy.wait()
+
+
+def finish(arrays):
+    count = len(arrays)
+    spec = pl.BlockSpec(memory_space=pl.ANY)
+    return pl.pallas_call(
+        functools.partial(finish_kernel, count),
+        out_shape=tuple(jax.ShapeDtypeStruct(a.shape, a.dtype) for a in arrays),
+        in_specs=[spec] * count,
+        out_specs=(spec,) * count,
+        scratch_shapes=[pltpu.VMEM(a.shape, a.dtype) for a in arrays] + [pltpu.SemaphoreType.DMA((2, count))],
+        compiler_params=pltpu.CompilerParams(vmem_limit_bytes=VMEM_LIMIT),
+    )(*arrays)
 
 
 def whole(shape=None):
@@ -530,7 +1215,19 @@
     cot = cotangent.reshape(rows, width)
     g1, g2, g3 = (gain.reshape(1, width) for gain in (gain_self, gain_cross, gain_feed))
     length_row = lengths.reshape(passages)
-    source = lax.all_to_all(encodings, "pass", split_axis=2, concat_axis=0, tiled=True).reshape(keys, width)
+    share = width // n
+    fits = passages == n and keys * width * 8 <= 16 << 20 and units == 4 * width
+    if n & (n - 1) == 0 and n >= 8 and share % 16 == 0 and fits:
+        out = layer(n, slot, Inputs(
+            length_row, encodings.reshape(n, slot, width), wq, wk, wv, wo, wcq, wck, wcv, wco, w_in, w_out, own, cot,
+            gain_self, gain_cross, gain_feed, table.T,
+        ))
+        out = finish(out)
+        rows_out = tuple(o.reshape(hidden.shape) for o in out[:2])
+        gains = tuple(gain.reshape(share) for gain in out[13:16])
+        return rows_out + (out[2].reshape(encodings.shape),) + tuple(out[3:13]) + gains + (out[16].T,)
+
+    source = lax.all_to_all(encodings, PASS, split_axis=2, concat_axis=0, tiled=True).reshape(keys, width)
 
     sixteen, wide = ((rows, width), BF), ((rows, width), F32)
     h1, q, k, v, mix1, after_self, h2, cq = call(
@@ -596,7 +1293,7 @@
         compiler_params=pltpu.CompilerParams(vmem_limit_bytes=VMEM_LIMIT),
     )(length_row, source, ck, cv, wck, wcv, cq, gmix, lse, delta)
     returned = lax.all_to_all(
-        enc_grad.reshape(passages, 1, 1, slot, width), "pass", split_axis=0, concat_axis=2, tiled=True
+        enc_grad.reshape(passages, 1, 1, slot, width), PASS, split_axis=0, concat_axis=2, tiled=True
     )
 
     gain_kind = ((1, width), F32)
@@ -607,33 +1304,16 @@
         own, h1, q, k, v, mix1, after_self, h2, dcq, grad_cross, wq, wk, wv, wo, wcq, g1, g2, table,
     )
 
-    share = width // n
-    if n & (n - 1) == 0 and share % 16 == 0:
-        squares = [d_q, d_k, d_v, d_so, d_cq, d_ck, d_cv, d_co]
-        parts = [d.reshape(n, share, width) for d in squares]
-        parts += [d_in[i].reshape(n, share, width) for i in range(pieces)]
-        big = d_out.reshape(n, pieces, share, width)
-        flat = jnp.concatenate([dg1, dg2, dg3, jnp.pad(dtable.reshape(1, -1), ((0, 0), (0, width - dtable.size))),
-                                jnp.zeros((4, width), F32)], axis=0)
-        sums, small = reduce_all(n, parts, big, flat)
-        totals = [sums[i] for i in range(8)]
-        count = len(squares)
-        in_total = jnp.concatenate([sums[count + i] for i in range(pieces)], axis=1)
-        out_total = sums[count + pieces :].reshape(pieces * share, width)
-        me = lax.axis_index("pass")
-        gains = [lax.dynamic_slice(small[i], (me * share,), (share,)) for i in range(3)]
-        table_sum = small[3, : dtable.size].reshape(table.shape)
-    else:
-        both = [d_q, d_k, d_v, d_so, d_cq, d_ck, d_cv, d_co, d_in.transpose(1, 0, 2).reshape(width, units), d_out]
-
-        def total(part):
-            shared = lax.psum_scatter(part, "pass", scatter_dimension=0, tiled=True)
-            return lax.psum(shared.astype(BF), "pb").astype(F32)
-
-        sums = [total(part.astype(F32)) for part in both]
-        totals, in_total, out_total = sums[:8], sums[8], sums[9]
-        gains = [total(part.reshape(width)) for part in (dg1, dg2, dg3)]
-        table_sum = lax.psum(dtable, ("pass", "pb"))
+    both = [d_q, d_k, d_v, d_so, d_cq, d_ck, d_cv, d_co, d_in.transpose(1, 0, 2).reshape(width, units), d_out]
+
+    def total(part):
+        shared = lax.psum_scatter(part, PASS, scatter_dimension=0, tiled=True)
+        return lax.psum(shared.astype(BF), CORE).astype(F32)
+
+    sums = [total(part.astype(F32)) for part in both]
+    totals, in_total, out_total = sums[:8], sums[8], sums[9]
+    gains = [total(part.reshape(width)) for part in (dg1, dg2, dg3)]
+    table_sum = lax.psum(dtable, (PASS, CORE))
     return (
         (result.reshape(hidden.shape), hidden_grad.reshape(hidden.shape), returned)
         + tuple(totals)
@@ -644,12 +1324,12 @@
 
 
 def solution(mesh):
-    rows = P("pb", "pass", None, None)
-    passage = P("pass", "pb", None, None, None)
-    in_specs = (rows, passage, P("pb", "pass", None), rows) + (P(),) * 14
-    out_specs = (rows, rows, passage) + (P("pass", None),) * 10 + (P("pass"),) * 3 + (P(),)
+    rows = P(CORE, PASS, None, None)
+    passage = P(PASS, CORE, None, None, None)
+    in_specs = (rows, passage, P(CORE, PASS, None), rows) + (P(),) * 14
+    out_specs = (rows, rows, passage) + (P(PASS, None),) * 10 + (P(PASS),) * 3 + (P(),)
     return jax.shard_map(
-        functools.partial(per_device, mesh.shape["pass"]),
+        functools.partial(per_device, mesh.shape[PASS]),
         mesh=mesh,
         in_specs=in_specs,
         out_specs=out_specs,

time: 378 us -> 212 us (0.56)
  Pallas kernels: 281 us -> 210 us
  waiting for transfers between devices: 62.4 us -> 0 us
  local copies, waits for them, and re-layouts: 20.5 us -> 0 us
  starting transfers between devices: 11.7 us -> 0 us
    pallas_call x6 -> x2, Pallas kernels: 281 us -> 210 us  [the longest x1 205 us: layer(): pl.pallas_call(functools.partial(layer_kernel, n, slot, count_in, count_o...]
    all_to_all x2 -> x0, waiting for transfers between devices: 62.4 us -> none  [the longest x1 62.4 us: per_device(): lax.all_to_all(encodings, 'pass', split_axis=2, concat_axis=0, tiled=True)]
    all_to_all x2 -> x0, starting transfers between devices: 11.7 us -> none  [the longest x1 6.75 us: per_device(): lax.all_to_all(encodings, 'pass', split_axis=2, concat_axis=0, tiled=True)]
    slice x4 -> x0, local copies, waits for them, and re-layouts: 8.11 us -> none  [the longest x1 4.61 us: per_device(): parts += [d_in[i].reshape(n, share, width) for i in range(pieces)]]
    unnamed x15 -> x0, local copies, waits for them, and re-layouts: 4.72 us -> none
  transfers between devices with their start and end apart: 2 -> 0, of which waited for: 1 -> 0; matrix products, arithmetic and copies ran while one was open for 5% -> 0% of each run, Pallas kernels for 59% -> 0%
where the time goes in v3:
time: 212 us; the launch traced here: 211 us
  Pallas kernels  210 us (99%)
    pallas_call x1, Pallas kernels, layer(): pl.pallas_call(functools.partial(layer_kernel, n, slot, count_in, count_o...  205 us
    pallas_call x1, Pallas kernels, finish(): pl.pallas_call(functools.partial(finish_kernel, count), out_shape=tuple((...  5.18 us

profile of v3, /device:TPU:13, one launch (start us, length us, event | category | flops | bytes accessed | tf_op | source)
XLA Modules:
  0.0 211.0 jit_solution(2903400940052608968)
XLA Ops:
  0.7 204.9 %shard_map.305 = (f32[128,768]{1,0:T(8,128)}, f32[128,768]{1,0:T(8,128)}, bf16[16,128,768]{2,1,0:T(8,128)(2,1)}, f32[48,768]{1,0:T(8,128)}, f32[48,768]{1,0:T(8,...) custom-call(s32[16]{0:T(128)} %bitcast.16, ...), custom_call_target="tpu_custom_call" | custom-call | tf_op jit(solution)/shard_map/pallas_call | solution.py:1154
  205.6 5.2 %shard_map.306 = (f32[128,768]{1,0:T(8,128)}, f32[128,768]{1,0:T(8,128)}, bf16[16,128,768]{2,1,0:T(8,128)(2,1)}, f32[48,768]{1,0:T(8,128)}, f32[48,768]{1,0:T(8,...) custom-call(f32[128,768]{1,0:T(8,128)} %get-tuple-element.51.refs_0_, ...), custom_call_target="tpu_custom_call" | custom-call | tf_op jit(solution)/shard_map/pallas_call | solution.py:1180

commit v4 on v3

--- a/solution.py
+++ b/solution.py
@@ -16,7 +16,7 @@
 F32 = jnp.float32
 MESH = pl.DeviceIdType.MESH
 PASS, CORE = "pass", "pb"
-PLANES_FIRST = (2, 3, 6, 7, 11)
+PLANES_FIRST = (2, 3, 6, 7, 13)
 ROOT = 0.7978845608028654
 VMEM_LIMIT = 56 << 20
 LAYER_LIMIT = 64 << 20
@@ -354,19 +354,10 @@
     result: Any
     hidden: Any
     enc: Any
-    sq: Any
-    sk: Any
-    sv: Any
-    so: Any
-    cq: Any
-    ck: Any
-    cv: Any
-    co: Any
+    squares: Any
     fin: Any
     fout: Any
-    gs: Any
-    gc: Any
-    gf: Any
+    gains: Any
     table: Any
 
 
@@ -400,8 +391,14 @@
     mine: Any
     last_own: Any
     last_other: Any
-    small_gains: Any
-    small_table: Any
+    out_result: Any
+    out_hidden: Any
+    out_squares: Any
+    out_fin: Any
+    out_fout: Any
+    small_give: Any
+    small_take: Any
+    small_sum: Any
     load: Any
     pair_send: Any
     pair_recv: Any
@@ -410,7 +407,9 @@
     in_send: Any
     in_recv: Any
     all_send: Any
-    all_recv: Any
+    line_recv: Any
+    first_recv: Any
+    plane_recv: Any
     own: Any
     out: Any
     small_send: Any
@@ -448,6 +447,12 @@
             src_ref=src, dst_ref=dst, send_sem=send, recv_sem=recv, device_id=device, device_id_type=MESH
         )
 
+    def all_sent(like, sem):
+        remote(like, like, sem, sem, partner).wait_send()
+
+    def all_come(like, sem):
+        remote(like, like, sem, sem, partner).wait_recv()
+
     def by_core(body):
         for c in range(2):
             pl.when(core == c)(functools.partial(body, c))
@@ -482,10 +487,10 @@
         return pl.ds(pl.multiple_of(p * slot, slot), slot)
 
     def bring(q):
-        return remote(ins.encodings.at[q], r.enc.at[passage_at(me)], r.in_send.at[q], r.in_recv.at[me], (q, core))
+        return remote(ins.encodings.at[q], r.enc.at[passage_at(me)], r.in_send.at[0], r.in_recv.at[me], (q, core))
 
     def arrived(p):
-        return remote(ins.encodings.at[p], r.enc.at[passage_at(p)], r.in_send.at[p], r.in_recv.at[p], (p, core))
+        return remote(ins.encodings.at[p], r.enc.at[passage_at(p)], r.in_send.at[0], r.in_recv.at[p], (p, core))
 
     def bring_range(first, last):
         def one(d, carry):
@@ -509,7 +514,7 @@
         last = k & -k
         origin = me ^ (4 * (k ^ last))
         ref = r.stats.at[origin] if kind == 2 else (r.queries, r.grads)[kind].at[:, origin]
-        return remote(ref, ref, r.all_send.at[kind, k - 1], r.all_recv.at[kind, k - 1], (me ^ (4 * last), core))
+        return remote(ref, ref, r.all_send.at[kind], r.line_recv.at[kind, k - 1], (me ^ (4 * last), core))
 
     def spread_line(kind, number):
         if number:
@@ -523,13 +528,12 @@
         first, second = (x_peer, y_peer) if part == 0 else (y_peer, x_peer)
         origin = me ^ (4 * k) if number < 4 else me ^ (4 * k) ^ (1 << part)
         at = (r.queries, r.grads)[kind].at[part, origin]
-        sem = line - 1 + number * line + k
-        return remote(at, at, r.all_send.at[kind, sem], r.all_recv.at[kind, sem], first if number < 2 else second)
+        recv = r.first_recv.at[kind, number, k] if number < 2 else r.plane_recv.at[kind]
+        return remote(at, at, r.all_send.at[kind], recv, first if number < 2 else second)
 
     def stat_plane(d):
         view = r.stats.reshape(line, 4, *r.stats.shape[1:]).at[:, low]
-        sem = line - 2 + d
-        return remote(view, view, r.all_send.at[2, sem], r.all_recv.at[2, sem], (me ^ d, core))
+        return remote(view, view, r.all_send.at[2], r.plane_recv.at[2], (me ^ d, core))
 
     def spread_plane(kind, blocks):
         for number in range(4):
@@ -545,16 +549,20 @@
                 plane_copy(kind, number, k).start()
 
     def spread_taken(kind):
-        for number in range(2, 6):
-            for k in range(line):
-                plane_copy(kind, number, k).wait_recv()
+        like = r.stats.at[: 3 * line] if kind == 2 else r.grads.at[:, : 2 * line]
+        all_come(like, r.plane_recv.at[kind])
 
     def spread_sent(kind):
-        for k in range(1, line):
-            line_copy(kind, k).wait_send()
-        for number in range(6):
-            for k in range(line):
-                plane_copy(kind, number, k).wait_send()
+        like = r.stats.at[: 4 * line - 1] if kind == 2 else r.grads.at[:, : 4 * line - 1]
+        all_sent(like, r.all_send.at[kind])
+
+    ready = (
+        (r.out_result, outs.result), (r.out_hidden, outs.hidden), (r.out_squares, outs.squares), (r.out_fin, outs.fin),
+        (r.out_fout, outs.fout),
+    )
+
+    def give_out(i):
+        return pltpu.make_async_copy(*ready[i], r.out.at[2 + i])
 
     value = ins.hidden[...].astype(F32)
     h1 = narrow(rms(value, g1))
@@ -613,23 +621,23 @@
     load(5).wait()
     load(6).wait()
     own_passage.wait()
-    few = 2
+    few = 1
     turns = n // few
 
     def forward_block(turn, carry):
-        @pl.when(turn == 1)
+        @pl.when(turn == turns // 8)
         def _():
             for number in range(1, line_bits):
                 spread_line(0, number)
             bring_range(3 * n // 4, n)
             bring_range(4, n // 2)
 
-        @pl.when(turn == 3)
+        @pl.when(turn == 3 * turns // 8)
         def _():
             spread_line(0, line_bits)
             spread_plane(0, range(line))
 
-        pl.when(turn == turns - 2)(functools.partial(spread_rest, 0, range(line)))
+        pl.when(turn == 3 * turns // 4)(functools.partial(spread_rest, 0, range(line)))
         part = turn // (turns // 4)
         moved = turn % (turns // 4) + (part % 2 * 2 + part // 2) * (turns // 4)
         first = (moved ^ (me // few)) * few
@@ -675,16 +683,25 @@
     cb = ins.cot[...]
     result = after_cross
     into = jnp.zeros((rows, width), F32)
+    products = {}
+
+    def ahead_of(j):
+        if j < parts:
+            load(8 + 2 * j).wait()
+            load(9 + 2 * j).wait()
+            products[j] = dot_nn(h3, tiles[j]), dot_nt(cb, tiles[parts + j])
+
+    ahead_of(0)
     for j in range(parts):
-        load(8 + 2 * j).wait()
-        inner = dot_nn(h3, tiles[j])
+        ahead_of(j + 1)
+        inner, back = products.pop(j)
         bent = jnp.tanh(ROOT * (inner + 0.044715 * (inner * inner * inner)))
         active = narrow(0.5 * inner * (1.0 + bent))
         r.left_feed[0, :, j * width : (j + 1) * width] = active
         slope = 0.5 * (1.0 + bent) + (0.5 * ROOT) * inner * (1.0 - bent * bent) * (1.0 + (3 * 0.044715) * inner * inner)
-        load(9 + 2 * j).wait()
+        gi = narrow(back * slope)
+        into = into + dot_nt(gi, tiles[j])
         result = result + dot_nn(active, tiles[parts + j])
-        gi = narrow(dot_nt(cb, tiles[parts + j]) * slope)
         to = slice((j % (parts // 2)) * width, (j % (parts // 2) + 1) * width)
 
         def keep(c, gi=gi, to=to, owner=j // (parts // 2)):
@@ -694,8 +711,8 @@
                 r.give[:, to] = gi
 
         by_core(keep)
-        into = into + dot_nt(gi, tiles[j])
-    outs.result[...] = result
+    r.out_result[...] = result
+    give_out(0).start()
     pair_copy(1).start()
     back, dg3 = rms_back(after_cross, g3, into)
     grad = cb.astype(F32) + back
@@ -752,23 +769,23 @@
     def stage_copy(piece, stage):
         half_of, value, inner, outer, bit = split(piece, stage)
         dst = stages[stage].at[piece].reshape(outer, inner, share, half)
-        sems = r.sum_send.at[piece, stage], r.sum_recv.at[piece, stage]
+        sems = r.sum_send.at[0], r.sum_recv.at[piece, stage]
         return remote(half_of(1 - value), dst, *sems, (me ^ (1 << bit), core))
 
     first_square = count_in + count_out
-    square_outs = (outs.co, outs.cq, outs.so, outs.sq, outs.sk, outs.sv, outs.ck, outs.cv)
+    square_places = (7, 4, 3, 0, 1, 2, 5, 6)
 
     def put(piece, c, total):
         if piece < count_in:
-            outs.fin[:, (c * count_in + piece) * half : (c * count_in + piece + 1) * half] = total
+            r.out_fin[:, (c * count_in + piece) * half : (c * count_in + piece + 1) * half] = total
         elif piece < first_square:
             k = piece - count_in
-            outs.fout[k * share : (k + 1) * share, c * half : (c + 1) * half] = total
+            r.out_fout[k * share : (k + 1) * share, c * half : (c + 1) * half] = total
         else:
-            square_outs[piece - first_square][:, c * half : (c + 1) * half] = total
+            r.out_squares[square_places[piece - first_square], :, c * half : (c + 1) * half] = total
 
     def last_copy(piece):
-        return remote(r.last_own.at[piece], r.last_other.at[piece], r.last_send.at[piece], r.last_recv.at[piece], partner)
+        return remote(r.last_own.at[piece], r.last_other.at[piece], r.last_send.at[0], r.last_recv.at[0], partner)
 
     def begin(piece):
         stage_copy(piece, 0).start()
@@ -846,7 +863,7 @@
     lefts = (width, 2 * width, 0, 0, 0)
 
     def late_copy(i):
-        return remote(r.late_give.at[i], r.late.at[i, 1], r.pair_send.at[3 + i], r.pair_recv.at[3 + i], partner)
+        return remote(r.late_give.at[i], r.late.at[i, 1], r.pair_send.at[3], r.pair_recv.at[3 + i], partner)
 
     def late_give(name, value):
         i = late.index(name)
@@ -919,44 +936,53 @@
     late_take(SK, False)
     late_take(SV, False)
     back, dg1 = rms_back(ins.hidden[...].astype(F32), g1, into)
-    outs.hidden[...] = grad + back
+    r.out_hidden[...] = grad + back
+    give_out(1).start()
     onehot = bucket_onehot_rows(ins.table.shape[1], rows)
     dtable = lax.dot_general(
         jnp.concatenate(sums, axis=0), onehot, (((1,), (1,)), ((), ())), precision=lax.Precision.HIGHEST,
         preferred_element_type=F32,
     )
 
-    small = (r.small_gains, r.small_table)
-
-    def small_copies(step):
-        device = partner if step == bits else (me ^ (1 << step), core)
-        return [
-            remote(ref.at[step], ref.at[bits + 1 + step], r.small_send.at[j, step], r.small_recv.at[j, step], device)
-            for j, ref in enumerate(small)
-        ]
-
-    r.small_gains[0] = jnp.concatenate([dg1, dg2, dg3, jnp.zeros((5, width), F32)], axis=0)
-    r.small_table[0] = jnp.zeros(r.small_table.shape[1:], F32)
-    r.small_table[0, : dtable.shape[0], : dtable.shape[1]] = dtable
-    for copy in small_copies(0):
-        copy.start()
-
-    def small_step(step):
-        for copy in small_copies(step):
-            copy.wait_recv()
-        gains, table = (ref[step] + ref[bits + 1 + step] for ref in small)
-        if step < bits:
-            r.small_gains[step + 1] = gains
-            r.small_table[step + 1] = table
-            for copy in small_copies(step + 1):
-                copy.start()
-        else:
-            outs.table[...] = table[: dtable.shape[0], : dtable.shape[1]]
-            for j, out in enumerate((outs.gs, outs.gc, outs.gf)):
-                own = jnp.zeros((1, share), F32)
-                for o in range(n):
-                    own = jnp.where(me == o, gains[j : j + 1, o * share : (o + 1) * share], own)
-                out[...] = own
+    heads, buckets = dtable.shape
+    per_row = 128 // buckets
+    table_rows = [
+        jnp.concatenate([dtable[i + j : i + j + 1] for j in range(per_row)], axis=1) for i in range(0, heads, per_row)
+    ]
+    terms = jnp.concatenate([dg1, dg2, dg3], axis=0)
+    for o in range(n):
+        r.small_give[o, :3, :share] = terms[:, o * share : (o + 1) * share]
+        r.small_give[o, 3 : 3 + len(table_rows)] = jnp.concatenate(table_rows, axis=0)
+    r.small_take[me] = r.small_give[me]
+
+    def small_copy(device):
+        return remote(r.small_give.at[device], r.small_take.at[me], r.small_send.at[0], r.small_recv.at[0], (device, core))
+
+    def small_one(d, carry):
+        small_copy(me ^ d).start()
+        return carry
+
+    lax.fori_loop(1, n, small_one, 0)
+
+    def small_pair():
+        return remote(r.small_sum.at[0], r.small_sum.at[1], r.small_send.at[1], r.small_recv.at[1], partner)
+
+    def small_add():
+        all_come(r.small_take.at[: n - 1], r.small_recv.at[0])
+        total = r.small_take[0]
+        for o in range(1, n):
+            total = total + r.small_take[o]
+        r.small_sum[0] = total
+        small_pair().start()
+
+    def small_end():
+        small_pair().wait_recv()
+        total = r.small_sum[0] + r.small_sum[1]
+        for i in range(3):
+            outs.gains[i] = total[i : i + 1, :share]
+        for i in range(len(table_rows)):
+            for j in range(per_row):
+                outs.table[i * per_row + j : i * per_row + j + 1] = total[3 + i : 4 + i, j * buckets : (j + 1) * buckets]
 
     place_f = place.astype(F32)
 
@@ -994,7 +1020,7 @@
         elif piece == first_square + SV:
             keys = (3.05, 3.85, 4.25, 4.75)
         elif piece == first_square + SK:
-            keys = (2.1, 3.35, 3.65, 4.65)
+            keys = (3.05, 3.58, 4.02, 4.65)
         else:
             keys = (2.0, 3.1, 3.6, 4.6)
         return keys[min(stage, 2)] if stage + 1 < bits else keys[3]
@@ -1010,10 +1036,8 @@
 
     spread_taken(0)
     spread_taken(1)
-    for d in range(1, 4):
-        stat_plane(d).wait_recv()
+    spread_taken(2)
     lax.fori_loop(line, 2 * line, owner_block, 0)
-    small_step(0)
     for piece, stage in visits[1]:
         arrive(piece, stage)
     lax.fori_loop(2 * line, n, owner_block, 0)
@@ -1030,11 +1054,11 @@
     def out_copy(c):
         return pltpu.make_async_copy(r.grads.at[c], outs.enc.at[:, :, c * half : (c + 1) * half], r.out.at[c])
 
-    spread_sent(0)
-    spread_sent(1)
+    for kind in range(3):
+        spread_sent(kind)
 
     def swap_copy(i):
-        return remote(r.swap_give.at[i], r.swap_take.at[i], r.pair_send.at[8 + i], r.pair_recv.at[8 + i], partner)
+        return remote(r.swap_give.at[i], r.swap_take.at[i], r.pair_send.at[4], r.pair_recv.at[8 + i], partner)
 
     def columns_of(ref, c):
         return owners(dot_tn(r.enc[...], ref[:, pl.ds(pl.multiple_of(c * half, 128), half)]))
@@ -1062,40 +1086,31 @@
             for c in range(2):
                 out_copy(c).start()
         arrive(piece, stage)
-        for step in range(1, bits + 1):
-            if (piece, stage) == (last[1], step - 1):
-                small_step(step)
-
+        if (piece, stage) == (last[1], 0):
+            small_add()
+    small_end()
+
+    all_come(r.last_other, r.last_recv.at[0])
     for piece in range(pieces):
-        last_copy(piece).wait_recv()
         total = r.last_other[piece].astype(F32)
         by_core(lambda c: put(piece, 1 - c, total))
-
+        if piece in (count_in - 1, first_square - 1, pieces - 1):
+            give_out(3 if piece < count_in else 4 if piece < first_square else 2).start()
+
+    for i in range(len(ready)):
+        give_out(i).wait()
     for c in range(2):
         out_copy(c).wait()
 
-    def brought(d, carry):
-        bring(me ^ d).wait_send()
-        return carry
-
-    lax.fori_loop(1, n, brought, 0)
-    for k in range(1, line):
-        line_copy(2, k).wait_send()
-    for d in range(1, 4):
-        stat_plane(d).wait_send()
+    all_sent(r.enc.at[: (n - 1) * slot], r.in_send.at[0])
     for i in range(3):
         pair_copy(i).wait_send()
-    for i in range(5):
-        late_copy(i).wait_send()
-    for i in range(2):
-        swap_copy(i).wait_send()
-    for piece in range(pieces):
-        for stage in range(bits):
-            stage_copy(piece, stage).wait_send()
-        last_copy(piece).wait_send()
-    for step in range(bits + 1):
-        for copy in small_copies(step):
-            copy.wait_send()
+    all_sent(r.late_give, r.pair_send.at[3])
+    all_sent(r.swap_give, r.pair_send.at[4])
+    all_sent(mine.at[:, : n - 1], r.sum_send.at[0])
+    all_sent(r.last_own, r.last_send.at[0])
+    all_sent(r.small_give.at[: n - 1], r.small_send.at[0])
+    all_sent(r.small_sum.at[0], r.small_send.at[1])
 
 
 def layer(n, slot, args):
@@ -1111,11 +1126,12 @@
     vmem, hbm = pl.BlockSpec(memory_space=pltpu.VMEM), pl.BlockSpec(memory_space=pl.ANY)
     in_specs = [pl.BlockSpec(memory_space=pltpu.SMEM)] + [hbm] * 11 + [vmem] * 6
     wide = jax.ShapeDtypeStruct((rows, width), F32)
-    square = jax.ShapeDtypeStruct((share, width), F32)
-    gain = jax.ShapeDtypeStruct((1, share), F32)
-    results = [wide, wide, jax.ShapeDtypeStruct((n, slot, width), BF)] + [square] * 8
-    results += [jax.ShapeDtypeStruct((share, units), F32), jax.ShapeDtypeStruct((count_out * share, width), F32)]
-    results += [gain] * 3 + [jax.ShapeDtypeStruct(table, F32)]
+    results = Outputs(
+        result=wide, hidden=wide, enc=jax.ShapeDtypeStruct((n, slot, width), BF),
+        squares=jax.ShapeDtypeStruct((8, share, width), F32), fin=jax.ShapeDtypeStruct((share, units), F32),
+        fout=jax.ShapeDtypeStruct((count_out * share, width), F32), gains=jax.ShapeDtypeStruct((3, 1, share), F32),
+        table=jax.ShapeDtypeStruct(table, F32),
+    )
     dma = pltpu.SemaphoreType.DMA
     sixteen, full = pltpu.VMEM((rows, width), BF), pltpu.VMEM((rows, width), F32)
     stat, masks = pltpu.VMEM((pairs, 2 * rows), F32), pltpu.VMEM((pairs, 2 * rows, 2 * HD), BF)
@@ -1123,6 +1139,7 @@
     swap = pltpu.VMEM((2, n, share, half), BF)
     last = pltpu.VMEM((pieces, share, half), BF)
     up = lambda count: -(-count // 8) * 8
+    small_rows = up(3 + table[0] * table[1] // 128)
     scratch = Scratch(
         left_self=pltpu.VMEM((2, rows, 3 * width), BF),
         left_feed=pltpu.VMEM((2, rows, units + 2 * width), BF),
@@ -1139,50 +1156,62 @@
         top=stat, lse=stat, delta=stat, swap_give=swap, swap_take=swap,
         mine=pltpu.VMEM((pieces // 2, n, share, width), BF),
         last_own=last, last_other=last,
-        small_gains=pltpu.VMEM((2 * (bits + 1), 8, width), F32),
-        small_table=pltpu.VMEM((2 * (bits + 1), up(table[0]), 128), F32),
+        out_result=full, out_hidden=full,
+        out_squares=pltpu.VMEM((8, share, width), F32),
+        out_fin=pltpu.VMEM((share, units), F32),
+        out_fout=pltpu.VMEM((count_out * share, width), F32),
+        small_give=pltpu.VMEM((n, small_rows, 128), F32), small_take=pltpu.VMEM((n, small_rows, 128), F32),
+        small_sum=pltpu.VMEM((2, small_rows, 128), F32),
         load=dma((8 + 2 * (units // width),)),
-        pair_send=dma((10,)), pair_recv=dma((10,)),
-        sum_send=dma((pieces, bits)), sum_recv=dma((pieces, bits)),
-        in_send=dma((n,)), in_recv=dma((n,)),
-        all_send=dma((3, 7 * (n // 4))), all_recv=dma((3, 7 * (n // 4))),
-        own=dma((1,)), out=dma((2,)),
-        small_send=dma((2, bits + 1)), small_recv=dma((2, bits + 1)),
-        last_send=dma((pieces,)), last_recv=dma((pieces,)),
+        pair_send=dma((5,)), pair_recv=dma((10,)),
+        sum_send=dma((1,)), sum_recv=dma((pieces, bits)),
+        in_send=dma((1,)), in_recv=dma((n,)),
+        all_send=dma((3,)), line_recv=dma((3, n // 4 - 1)), first_recv=dma((2, 2, n // 4)), plane_recv=dma((3,)),
+        own=dma((1,)), out=dma((7,)),
+        small_send=dma((2,)), small_recv=dma((2,)),
+        last_send=dma((1,)), last_recv=dma((1,)),
     )
     stages = [pltpu.VMEM((pieces, n >> (b + 1), share, half), BF) for b in range(bits)]
     return pl.pallas_call(
         functools.partial(layer_kernel, n, slot, count_in, count_out),
         out_shape=tuple(results),
         in_specs=in_specs,
-        out_specs=tuple([vmem, vmem, hbm] + [vmem] * 14),
+        out_specs=tuple([hbm] * 6 + [vmem] * 2),
         scratch_shapes=list(scratch) + stages,
         compiler_params=pltpu.CompilerParams(collective_id=1, has_side_effects=True, vmem_limit_bytes=LAYER_LIMIT),
     )(*args)
 
 
-def finish_kernel(count, *refs):
-    ins, outs, held, sems = refs[:count], refs[count : 2 * count], refs[2 * count : 3 * count], refs[-1]
-    into = [pltpu.make_async_copy(ins[i], held[i], sems.at[0, i]) for i in range(count)]
-    back = [pltpu.make_async_copy(held[i], outs[i], sems.at[1, i]) for i in range(count)]
+def finish_kernel(parts, *refs):
+    count, total = len(parts), sum(parts)
+    ins, outs, held, sems = refs[:count], refs[count : count + total], refs[count + total : -1], refs[-1]
+    into = [pltpu.make_async_copy(ins[i], held[i], sems.at[i]) for i in range(count)]
     for copy in into:
         copy.start()
+    back = []
     for i in range(count):
         into[i].wait()
-        back[i].start()
+        for part in range(parts[i]):
+            number = len(back)
+            src = held[i] if parts[i] == 1 else held[i].at[part]
+            back.append(pltpu.make_async_copy(src, outs[number], sems.at[count + number]))
+            back[-1].start()
     for copy in back:
         copy.wait()
 
 
-def finish(arrays):
-    count = len(arrays)
+def finish(arrays, parts):
+    count, total = len(arrays), sum(parts)
     spec = pl.BlockSpec(memory_space=pl.ANY)
+    shapes = []
+    for array, part in zip(arrays, parts):
+        shapes += [jax.ShapeDtypeStruct(array.shape[part > 1 :], array.dtype)] * part
     return pl.pallas_call(
-        functools.partial(finish_kernel, count),
-        out_shape=tuple(jax.ShapeDtypeStruct(a.shape, a.dtype) for a in arrays),
+        functools.partial(finish_kernel, parts),
+        out_shape=tuple(shapes),
         in_specs=[spec] * count,
-        out_specs=(spec,) * count,
-        scratch_shapes=[pltpu.VMEM(a.shape, a.dtype) for a in arrays] + [pltpu.SemaphoreType.DMA((2, count))],
+        out_specs=(spec,) * total,
+        scratch_shapes=[pltpu.VMEM(a.shape, a.dtype) for a in arrays] + [pltpu.SemaphoreType.DMA((count + total,))],
         compiler_params=pltpu.CompilerParams(vmem_limit_bytes=VMEM_LIMIT),
     )(*arrays)
 
@@ -1217,15 +1246,19 @@
     length_row = lengths.reshape(passages)
     share = width // n
     fits = passages == n and keys * width * 8 <= 16 << 20 and units == 4 * width
-    if n & (n - 1) == 0 and n >= 8 and share % 16 == 0 and fits:
+    tables = 128 % table.shape[0] == 0 and table.size % 128 == 0
+    if n & (n - 1) == 0 and n >= 8 and share % 16 == 0 and share <= 128 and fits and tables:
         out = layer(n, slot, Inputs(
             length_row, encodings.reshape(n, slot, width), wq, wk, wv, wo, wcq, wck, wcv, wco, w_in, w_out, own, cot,
             gain_self, gain_cross, gain_feed, table.T,
         ))
-        out = finish(out)
-        rows_out = tuple(o.reshape(hidden.shape) for o in out[:2])
-        gains = tuple(gain.reshape(share) for gain in out[13:16])
-        return rows_out + (out[2].reshape(encodings.shape),) + tuple(out[3:13]) + gains + (out[16].T,)
+        result, hidden_grad, enc_grad, *sums, table_sum = finish(out, (1, 1, 1, 8, 1, 1, 3, 1))
+        return (
+            (result.reshape(hidden.shape), hidden_grad.reshape(hidden.shape), enc_grad.reshape(encodings.shape))
+            + tuple(sums[:10])
+            + tuple(gain.reshape(share) for gain in sums[10:])
+            + (table_sum.T,)
+        )
 
     source = lax.all_to_all(encodings, PASS, split_axis=2, concat_axis=0, tiled=True).reshape(keys, width)
 

time: 212 us -> 206 us (0.972)
  Pallas kernels: 210 us -> 202 us
    pallas_call x1, Pallas kernels: 205 us -> 197 us  [layer(): pl.pallas_call(functools.partial(layer_kernel, n, slot, count_in, count_o...]
where the time goes in v4:
time: 206 us; the launch traced here: 203 us
  Pallas kernels  202 us (98%)
    pallas_call x1, Pallas kernels, layer(): pl.pallas_call(functools.partial(layer_kernel, n, slot, count_in, count_o...  197 us
    pallas_call x1, Pallas kernels, finish(): pl.pallas_call(functools.partial(finish_kernel, parts), out_shape=tuple(s...  5.08 us

profile of v4, /device:TPU:13, one launch (start us, length us, event | category | flops | bytes accessed | tf_op | source)
XLA Modules:
  0.0 203.2 jit_solution(3496368766901291973)
XLA Ops:
  0.7 197.3 %shard_map.305 = (f32[128,768]{1,0:T(8,128)}, f32[128,768]{1,0:T(8,128)}, bf16[16,128,768]{2,1,0:T(8,128)(2,1)}, f32[8,48,768]{2,1,0:T(8,128)}, f32[48,3072]{1,0...) custom-call(s32[16]{0:T(128)} %bitcast.16, bf16[16,128,768]{2,1,0:T(8,128)(2,1)} %bitcast.12, ...), custom_call_target="tpu_custom_call" | custom-call | tf_op jit(solution)/shard_map/pallas_call | solution.py:1175
  197.9 5.1 %shard_map.306 = (f32[128,768]{1,0:T(8,128)}, f32[128,768]{1,0:T(8,128)}, bf16[16,128,768]{2,1,0:T(8,128)(2,1)}, f32[48,768]{1,0:T(8,128)}, f32[48,768]{1,0:T(8,...) custom-call(f32[128,768]{1,0:T(8,128)} %get-tuple-element.42.refs_0_, ...), custom_call_target="tpu_custom_call" | custom-call | tf_op jit(solution)/shard_map/pallas_call | solution.py:1209

commit v5 on v4

--- a/solution.py
+++ b/solution.py
@@ -785,7 +785,8 @@
             r.out_squares[square_places[piece - first_square], :, c * half : (c + 1) * half] = total
 
     def last_copy(piece):
-        return remote(r.last_own.at[piece], r.last_other.at[piece], r.last_send.at[0], r.last_recv.at[0], partner)
+        recv = r.last_recv.at[int(piece >= first_square)]
+        return remote(r.last_own.at[piece], r.last_other.at[piece], r.last_send.at[0], recv, partner)
 
     def begin(piece):
         stage_copy(piece, 0).start()
@@ -1078,6 +1079,12 @@
         lax.fori_loop(0, n, one, 0)
         begin(piece)
 
+    def take_other(group, members):
+        all_come(r.last_other.at[members.start : members.stop], r.last_recv.at[group])
+        for piece in members:
+            total = r.last_other[piece].astype(F32)
+            by_core(lambda c: put(piece, 1 - c, total))
+
     rest = visits[3]
     for number, (piece, stage) in enumerate(rest):
         if (piece, stage) == (last[0], 0):
@@ -1088,14 +1095,14 @@
         arrive(piece, stage)
         if (piece, stage) == (last[1], 0):
             small_add()
+        if (piece, stage) == (last[0], bits - 1):
+            take_other(0, range(first_square))
+            give_out(3).start()
+            give_out(4).start()
     small_end()
 
-    all_come(r.last_other, r.last_recv.at[0])
-    for piece in range(pieces):
-        total = r.last_other[piece].astype(F32)
-        by_core(lambda c: put(piece, 1 - c, total))
-        if piece in (count_in - 1, first_square - 1, pieces - 1):
-            give_out(3 if piece < count_in else 4 if piece < first_square else 2).start()
+    take_other(1, range(first_square, pieces))
+    give_out(2).start()
 
     for i in range(len(ready)):
         give_out(i).wait()
@@ -1169,7 +1176,7 @@
         all_send=dma((3,)), line_recv=dma((3, n // 4 - 1)), first_recv=dma((2, 2, n // 4)), plane_recv=dma((3,)),
         own=dma((1,)), out=dma((7,)),
         small_send=dma((2,)), small_recv=dma((2,)),
-        last_send=dma((1,)), last_recv=dma((1,)),
+        last_send=dma((1,)), last_recv=dma((2,)),
     )
     stages = [pltpu.VMEM((pieces, n >> (b + 1), share, half), BF) for b in range(bits)]
     return pl.pallas_call(

time: 206 us -> 206 us (level)
  no operation moved by 1% of the time
where the time goes in v5:
time: 206 us; the launch traced here: 203 us
  Pallas kernels  202 us (98%)
    pallas_call x1, Pallas kernels, layer(): pl.pallas_call(functools.partial(layer_kernel, n, slot, count_in, count_o...  197 us
    pallas_call x1, Pallas kernels, finish(): pl.pallas_call(functools.partial(finish_kernel, parts), out_shape=tuple(s...  5.08 us

profile of v5, /device:TPU:13, one launch (start us, length us, event | category | flops | bytes accessed | tf_op | source)
XLA Modules:
  0.0 202.8 jit_solution(17280267969243796995)
XLA Ops:
  0.7 196.9 %shard_map.305 = (f32[128,768]{1,0:T(8,128)}, f32[128,768]{1,0:T(8,128)}, bf16[16,128,768]{2,1,0:T(8,128)(2,1)}, f32[8,48,768]{2,1,0:T(8,128)}, f32[48,3072]{1,0...) custom-call(s32[16]{0:T(128)} %bitcast.16, bf16[16,128,768]{2,1,0:T(8,128)(2,1)} %bitcast.12, ...), custom_call_target="tpu_custom_call" | custom-call | tf_op jit(solution)/shard_map/pallas_call | solution.py:1182
  197.6 5.1 %shard_map.306 = (f32[128,768]{1,0:T(8,128)}, f32[128,768]{1,0:T(8,128)}, bf16[16,128,768]{2,1,0:T(8,128)(2,1)}, f32[48,768]{1,0:T(8,128)}, f32[48,768]{1,0:T(8,...) custom-call(f32[128,768]{1,0:T(8,128)} %get-tuple-element.42.refs_0_, ...), custom_call_target="tpu_custom_call" | custom-call | tf_op jit(solution)/shard_map/pallas_call | solution.py:1216
